TPU v7x, 128 devices: a whole 4x4x4 slice. The times are simulated.
128 devices in a mesh: bin: 8 (over z_hi, y), row: 4 (over x), col: 4 (over z_lo, core).
Axes of the slice: x: 4, y: 4, z: 4 (z_hi: 2, z_lo: 2; z = z_hi * 2 + z_lo), core: 2. Of those that a mesh axis runs over, the one named last changes fastest.
Arguments:
- snapshots: bfloat16 [4096, 64, 64], P('row', 'bin', 'col'), may hold values from -6 to 6
- focus_in: bfloat16 [64, 4096, 128], P('bin', 'row'), may hold values from -0.09375 to 0.09375
- focus_out: bfloat16 [64, 4096, 128], P('bin', 'row'), may hold values from -0.5 to 0.5
- start_basis: float32 [4096, 128], replicated, may hold values from -6 to 6
Outputs:
- covariance: float32 [4096, 4096], P('col', 'row')
- basis_out: float32 [4096, 128], P(('row', 'col'))
All inputs are finite; a program needn't handle non-finite values.
Results may differ from a plain program's by a relative error of at most 0.0045.
Values may be sent and summed in bfloat16 or wider, within the bound.
A program may use at most 128 MiB of HBM per device.

v0:
```python
import math

import jax
import jax.numpy as jnp
from jax import lax
from jax.sharding import PartitionSpec as P

ITERS = 2


def shards(snapshots, focus_in, focus_out, start_basis):
    rows_here, bins_here, snaps_here = snapshots.shape
    bin_count = lax.axis_size("bin")
    row_count = lax.axis_size("row")
    col_count = lax.axis_size("col")
    col_here = lax.axis_index("col")
    row_here = lax.axis_index("row")
    partial_proj = jnp.einsum(
        "mbs,bmr->brs", snapshots, focus_in, preferred_element_type=jnp.float32
    )
    projected = lax.psum(partial_proj, "row").astype(jnp.bfloat16)
    lifted = jnp.einsum("bmr,brs->mbs", focus_out, projected, preferred_element_type=jnp.float32)
    focused = (snapshots.astype(jnp.float32) + lifted).astype(jnp.bfloat16)
    columns = bins_here * snaps_here
    local_rows = focused.reshape(rows_here, columns)
    all_rows = lax.all_gather(local_rows, "row", axis=0, tiled=True)
    array_size = all_rows.shape[0]
    col_block = array_size // col_count
    piece_rows = col_block // bin_count
    scaling = 1.0 / (columns * col_count * bin_count)
    permuted = (
        all_rows.reshape(col_count, bin_count, piece_rows, columns)
        .transpose(1, 0, 2, 3)
        .reshape(array_size, columns)
    )
    share_rows = lax.psum_scatter(
        lax.dot_general(
            permuted, local_rows, (((1,), (1,)), ((), ())), preferred_element_type=jnp.float32
        ),
        ("bin", "col"),
        scatter_dimension=0,
        tiled=True,
    )
    tile_block = lax.all_gather(share_rows, "bin", axis=0, tiled=True)
    covariance = tile_block * scaling
    basis_now = start_basis
    for sweep_index in range(ITERS):
        col_rows = lax.dynamic_slice_in_dim(basis_now, col_here * col_block, col_block, 0)
        partial_image = lax.dot_general(
            covariance,
            col_rows,
            (((0,), (0,)), ((), ())),
            precision=lax.Precision.HIGHEST,
            preferred_element_type=jnp.float32,
        )
        row_sums = lax.psum(partial_image, "col")
        full_image = lax.all_gather(row_sums, "row", axis=0, tiled=True)
        gram_matrix = jnp.dot(
            full_image.T,
            full_image,
            precision=lax.Precision.HIGHEST,
            preferred_element_type=jnp.float32,
        )
        lower_factor = jnp.linalg.cholesky(gram_matrix)
        basis_now = jax.scipy.linalg.solve_triangular(lower_factor, full_image.T, lower=True).T
    out_rows = array_size // (row_count * col_count)
    mine_start = (row_here * col_count + col_here) * out_rows
    basis_out = lax.dynamic_slice_in_dim(basis_now, mine_start, out_rows, 0) * math.sqrt(array_size)
    return (covariance, basis_out)


def solution(mesh):
    in_specs = (P("row", "bin", "col"), P("bin", "row", None), P("bin", "row", None), P())
    out_specs = (P("col", "row"), P(("row", "col"), None))
    return jax.shard_map(shards, mesh=mesh, in_specs=in_specs, out_specs=out_specs, check_vma=False)
```

profile of v0, /device:TPU:1, one launch (start us, length us, event | category | flops | bytes accessed | tf_op | source)
XLA Modules:
  0.0 558.8 jit_solution(16705941478910044841)
XLA Ops:
  7.2 0.0 copy-start
  7.2 0.0 all-gather.5.cloned.1.call-start
  7.2 2.2 fusion.24
  9.4 14.6 %psum.21 = bf16[8,128,16]{1,2,0:T(8,128)(2,1)S(1)} all-reduce(f32[8,128,16]{1,2,0:T(8,128)S(1)} %fusion.24), channel_id=1, replica_groups=mesh['bin'=8,'row'=4,'col'=4] {'row'}, use_global_device_ids=true, to_apply=%region_0.0 | all-reduce | flops 16384 | bytes 98304 | tf_op jit(solution)/shard_map/psum | solution.py:21
  24.1 0.6 fusion.5
  24.7 0.9 copy.12
  25.6 0.0 all-gather.5.cloned.1.call-update
  25.6 0.0 reduce-scatter.2.cloned.1.call-start
  25.6 27.7 %all-gather.5.cloned.1.call-done = bf16[4096,128]{1,0:T(8,128)(2,1)} async-done(((bf16[1024,128]{1,0:T(8,128)(2,1)}), bf16[4096,128]{1,0:T(8,128)(2,1)}) %all-gather.5.cloned.1.call-update) | async-done | bytes 1048592 | tf_op jit(solution)/shard_map/all_gather | solution.py:26
  53.3 1.3 copy.13
  54.7 8.0 %fusion.21 = f32[4096,1024]{1,0:T(8,128)} fusion(bf16[4096,128]{1,0:T(8,128)(2,1)S(1)} %bitcast.49, bf16[1024,128]{0,1:T(8,128)(2,1)S(1)} %bitcast.51), kind=kOutput, calls=%fused_computation.33 | convolution fusion | flops 1073741824 | bytes 18087936 | tf_op jit(solution)/shard_map/dot_general | solution.py:37
  62.7 0.0 reduce-scatter.2.cloned.1.call-update
  62.7 0.0 all-gather.7.cloned.1.call-start
  62.8 184.6 %reduce-scatter.2.cloned.1.call-done = f32[128,1024]{1,0:T(8,128)} async-done(((f32[4096,1024]{1,0:T(8,128)}), f32[128,1024]{1,0:T(8,128)}) %reduce-scatter.2.cloned.1.call-update) | async-done | bytes 524304 | tf_op jit(solution)/shard_map/reduce_scatter | solution.py:36
  247.4 0.0 all-gather.7.cloned.1.call-update
  247.4 0.0 all-reduce.3.cloned.1.call-start
  247.5 77.1 %all-gather.7.cloned.1.call-done = f32[1024,1024]{1,0:T(8,128)} async-done(((f32[128,1024]{1,0:T(8,128)}), f32[1024,1024]{1,0:T(8,128)}) %all-gather.7.cloned.1.call-update) | async-done | bytes 4194320 | tf_op jit(solution)/shard_map/all_gather | solution.py:44
  324.6 2.6 broadcast_multiply_fusion
  327.2 0.0 copy-start.1
  327.2 2.0 copy-done.1
  329.2 8.5 %fusion.8 = f32[1024,128]{1,0:T(8,128)} fusion(f32[1024,1024]{1,0:T(8,128)S(1)} %broadcast_multiply_fusion, f32[4096,128]{1,0:T(8,128)} %param.10, s32[]{:T(128)S(6)} %select_n.10), kind=kOutput, calls=%fused_computation.10 | convolution fusion | flops 1610612736 | bytes 5242884 | tf_op jit(solution)/shard_map/dot_general | solution.py:49
  337.7 0.0 all-reduce.3.cloned.1.call-update
  337.8 0.0 all-gather.9.cloned.1.call-start
  337.8 36.4 %all-reduce.3.cloned.1.call-done = f32[1024,128]{1,0:T(8,128)} async-done(((f32[1024,128]{1,0:T(8,128)}), f32[1024,128]{1,0:T(8,128)}) %all-reduce.3.cloned.1.call-update) | async-done | bytes 524304 | tf_op jit(solution)/shard_map/psum | solution.py:56
  374.3 0.0 all-gather.9.cloned.1.call-update
  374.3 0.2 all-reduce.5.cloned.1.call-start
  374.5 32.6 %all-gather.9.cloned.1.call-done = f32[4096,128]{1,0:T(8,128)} async-done(((f32[1024,128]{1,0:T(8,128)}), f32[4096,128]{1,0:T(8,128)}) %all-gather.9.cloned.1.call-update) | async-done | bytes 2097168 | tf_op jit(solution)/shard_map/all_gather | solution.py:57
  407.1 5.7 %fusion.22 = f32[128,128]{1,0:T(8,128)S(1)} fusion(f32[4096,128]{1,0:T(8,128)} %all-gather.9.cloned.1.call-done), kind=kOutput, calls=%fused_computation.34 | convolution fusion | flops 805306368 | bytes 2162688 | tf_op jit(solution)/shard_map/dot_general | solution.py:58
  412.8 0.1 copy.14
  412.9 11.7 %cholesky.44 = f32[128,128]{1,0:T(8,128)S(1)} custom-call(f32[128,128]{1,0:T(8,128)S(1)} %fusion.15), custom_call_target="Cholesky" | custom-call | tf_op jit(solution)/shard_map/jit(cholesky)/cholesky | solution.py:64
  424.6 0.6 compare_reduce_fusion.1
  425.3 0.7 fusion.10
  425.9 9.8 %custom-call.6 = f32[1,128,128]{1,2,0:T(8,128)S(1)} custom-call(f32[1,128,128]{2,1,0:T(8,128)S(1)} %fusion.10), custom_call_target="InvertDiagBlocksLowerTriangular" | custom-call | tf_op jit(solution)/shard_map/jit(_solve_triangular)/triangular_solve | solution.py:65
  435.8 3.7 fusion.2
  439.4 7.8 %fusion.6 = f32[1024,128]{1,0:T(8,128)} fusion(f32[1024,1024]{1,0:T(8,128)S(1)} %copy-done.2, f32[128,4096]{1,0:T(8,128)S(1)} %fusion.2, s32[]{:T(128)S(6)} %select_n.10), kind=kOutput, calls=%fused_computation.8 | convolution fusion | flops 1610612736 | bytes 5242884 | tf_op jit(solution)/shard_map/dot_general | solution.py:49
  447.2 0.0 all-reduce.5.cloned.1.call-update
  447.3 0.0 all-gather.11.cloned.1.call-start
  447.3 38.3 %all-reduce.5.cloned.1.call-done = f32[1024,128]{1,0:T(8,128)} async-done(((f32[1024,128]{1,0:T(8,128)}), f32[1024,128]{1,0:T(8,128)}) %all-reduce.5.cloned.1.call-update) | async-done | bytes 524304 | tf_op jit(solution)/shard_map/psum | solution.py:56
  485.6 0.0 all-gather.11.cloned.1.call-update
  485.6 33.0 %all-gather.11.cloned.1.call-done = f32[4096,128]{1,0:T(8,128)} async-done(((f32[1024,128]{1,0:T(8,128)}), f32[4096,128]{1,0:T(8,128)}) %all-gather.11.cloned.1.call-update) | async-done | bytes 2097168 | tf_op jit(solution)/shard_map/all_gather | solution.py:57
  518.6 5.7 %fusion.23 = f32[128,128]{1,0:T(8,128)S(1)} fusion(f32[4096,128]{1,0:T(8,128)} %all-gather.11.cloned.1.call-done), kind=kOutput, calls=%fused_computation.35 | convolution fusion | flops 805306368 | bytes 2162688 | tf_op jit(solution)/shard_map/dot_general | solution.py:58
  524.3 0.1 copy.15
  524.4 11.7 %cholesky.55 = f32[128,128]{1,0:T(8,128)S(1)} custom-call(f32[128,128]{1,0:T(8,128)S(1)} %fusion.13), custom_call_target="Cholesky" | custom-call | tf_op jit(solution)/shard_map/jit(cholesky)/cholesky | solution.py:64
  536.1 0.6 compare_reduce_fusion
  536.8 0.7 fusion.11
  537.4 9.8 %custom-call.7 = f32[1,128,128]{1,2,0:T(8,128)S(1)} custom-call(f32[1,128,128]{2,1,0:T(8,128)S(1)} %fusion.11), custom_call_target="InvertDiagBlocksLowerTriangular" | custom-call | tf_op jit(solution)/shard_map/jit(_solve_triangular)/triangular_solve | solution.py:65
  547.3 3.5 fusion
  550.8 0.8 copy.16
  (10 shorter events, 0.1 us)
Async XLA Ops:
  7.2 16.9 %copy-start = (bf16[8,1024,128]{2,1,0:T(8,128)(2,1)S(1)}, bf16[8,1024,128]{2,1,0:T(8,128)(2,1)}, u32[]{:S(2)}) copy-start(bf16[8,1024,128]{2,1,0:T(8,128)(2,1)} %param.9) | copy-start | bytes 6291460
  7.2 16.9 %copy-start.3 = (bf16[1024,8,16]{0,2,1:T(8,128)(2,1)S(1)}, bf16[1024,8,16]{0,2,1:T(8,128)(2,1)}, u32[]{:S(2)}) copy-start(bf16[1024,8,16]{0,2,1:T(8,128)(2,1)} %param.7) | copy-start | bytes 786436
  7.2 46.2 %all-gather.5.cloned.1.call-start = ((), (), s32[]{:S(2)}) async-start(), calls=%async_computation.1 | async-start | bytes 1310720 | tf_op jit(solution)/shard_map/all_gather | solution.py:26
  25.6 221.8 %reduce-scatter.2.cloned.1.call-start = ((), (), s32[]{:S(2)}) async-start(), calls=%async_computation.2 | async-start | bytes 17301504 | tf_op jit(solution)/shard_map/reduce_scatter | solution.py:36
  62.7 261.8 %all-gather.7.cloned.1.call-start = ((), (), s32[]{:S(2)}) async-start(), calls=%async_computation.3 | async-start | bytes 4718592 | tf_op jit(solution)/shard_map/all_gather | solution.py:44
  247.4 126.8 %all-reduce.3.cloned.1.call-start = ((), (), s32[]{:S(2)}) async-start(), calls=%async_computation.4 | async-start | bytes 1048576 | tf_op jit(solution)/shard_map/psum | solution.py:56
  327.2 2.0 copy-start.1
  337.8 69.3 %all-gather.9.cloned.1.call-start = ((), (), s32[]{:S(2)}) async-start(), calls=%async_computation.5 | async-start | bytes 2621440 | tf_op jit(solution)/shard_map/all_gather | solution.py:57
  374.3 111.3 %all-reduce.5.cloned.1.call-start = ((), (), s32[]{:S(2)}) async-start(), calls=%async_computation.6 | async-start | bytes 1048576 | tf_op jit(solution)/shard_map/psum | solution.py:56
  435.7 3.7 copy-start.2
  447.3 71.3 %all-gather.11.cloned.1.call-start = ((), (), s32[]{:S(2)}) async-start(), calls=%async_computation.7 | async-start | bytes 2621440 | tf_op jit(solution)/shard_map/all_gather | solution.py:57
Sparse Core Ops, SparseCore 0:
  25.7 27.5 all-gather.4
  62.9 184.4 reduce-scatter.1
  249.7 74.8 all-gather.6
  337.9 36.3 all-reduce.2
  375.8 31.2 all-gather.8
  447.4 38.1 all-reduce.4
  487.3 31.2 all-gather.10
where the time goes:
time: 567 us; the launch traced here: 559 us
  waiting for transfers between devices  430 us (76%)
  other arithmetic  48.4 us (9%)
  matrix products  45.7 us (8%)
  between operations  14.7 us (3%)
  blocking collectives  14.6 us (3%)
    reduce_scatter x1, waiting for transfers between devices, shards(): lax.psum_scatter(lax.dot_general(permuted, local_rows, (((1,), (1,)), (()...  185 us
    all_gather x1, waiting for transfers between devices, shards(): tile_block = lax.all_gather(share_rows, 'bin', axis=0, tiled=True)  77.1 us
    psum x2, waiting for transfers between devices, shards(): row_sums = lax.psum(partial_image, 'col')  74.7 us
    all_gather x2, waiting for transfers between devices, shards(): full_image = lax.all_gather(row_sums, 'row', axis=0, tiled=True)  65.5 us
    all_gather x1, waiting for transfers between devices, shards(): all_rows = lax.all_gather(local_rows, 'row', axis=0, tiled=True)  27.7 us
    another operation x6, other arithmetic, shards(): lower_factor = jnp.linalg.cholesky(gram_matrix)  24.8 us
    another operation x4, other arithmetic, shards(): jax.scipy.linalg.solve_triangular(lower_factor, full_image.T, lower=True)  20.9 us
    dot_general x2, matrix products, shards(): lax.dot_general(covariance, col_rows, (((0,), (0,)), ((), ())), precision...  16.3 us
  transfers between devices with their start and end apart: 7, of which 7 were waited for; matrix products, arithmetic and copies ran while one was open for 0% of the time, Pallas kernels for 0%

commit v1 on v0

v1 whole, which is shorter than its diff:
```python
import functools
import math

import jax
import jax.numpy as jnp
from jax import lax
from jax.experimental import pallas as pl
from jax.experimental.pallas import tpu as pltpu
from jax.sharding import PartitionSpec as P

MESH = pl.DeviceIdType.MESH
HI = lax.Precision.HIGHEST
F32 = jnp.float32
BF16 = jnp.bfloat16


def mod4(v):
    return lax.rem(v + 4, 4)


def dot(a, b, ca, cb, precision=None):
    return lax.dot_general(a, b, (((ca,), (cb,)), ((), ())), precision=precision, preferred_element_type=F32)


def invert_factor(work):
    rows = lax.broadcasted_iota(jnp.int32, (128, 128), 0)
    lanes = lax.broadcasted_iota(jnp.int32, (128, 128), 1)
    lane1 = lax.broadcasted_iota(jnp.int32, (1, 128), 1)

    def step(j, carry):
        row = work[pl.ds(j, 1), :]
        now = work[...]
        col = jnp.sum(jnp.where(lanes == j, now, 0.0), axis=1, keepdims=True)
        pivot = jnp.sum(jnp.where(lane1 == j, row, 0.0), axis=1, keepdims=True)
        mult = jnp.where(rows > j, col / pivot, 0.0)
        row = jnp.where(lane1 == j, 1.0, row)
        work[...] = jnp.where((lanes == j) & (rows > j), 0.0, now) - mult * row
        return carry

    lax.fori_loop(0, 128, step, 0)


def apply_factor(work, block):
    rows = lax.broadcasted_iota(jnp.int32, (128, 128), 0)
    lanes = lax.broadcasted_iota(jnp.int32, (128, 128), 1)
    now = work[...]
    pivots = jnp.sum(jnp.where(rows == lanes, now, 0.0), axis=0, keepdims=True)
    inverse = jnp.where(rows > lanes, now, jnp.where(rows == lanes, 1.0, 0.0))
    return dot(block, inverse, 1, 1, HI) * lax.rsqrt(pivots)


def kernel(
    snap_hbm, fi_hbm, fo_hbm, x0_hbm, cov_ref, basis_ref,
    snap, fi, fo, x0, proj, full, slab, acc, sibc, piece, img, part, sibp, scat, zall,
    gpart, gsib, gown, gscat, gram, gpart2, gscat2, gram2, in_sem,
    p_s, p_r, g_s, g_r, a_s, a_r, x_s, x_r, c_s, c_r, v_s, v_r, i_s, i_r, q_s, q_r, r_s, r_r, z_s, z_r,
    gs_s, gs_r, ga_s, ga_r, gb_s, gb_r, l_sem,
):
    b = lax.axis_index("bin")
    x = lax.axis_index("row")
    c = lax.axis_index("col")
    k = lax.rem(c, 2)
    zl = c // 2
    y = lax.rem(b, 4)
    zh = b // 4
    z = zh * 2 + zl

    def at(x_, y_, z_, k_):
        return {"bin": (z_ // 2) * 4 + y_, "row": x_, "col": lax.rem(z_, 2) * 2 + k_}

    sibling = at(x, y, z, 1 - k)

    def rdma(src, dst, s, r, device):
        return pltpu.make_async_remote_copy(
            src_ref=src, dst_ref=dst, send_sem=s, recv_sem=r, device_id=device, device_id_type=MESH
        )

    loads = [
        pltpu.make_async_copy(snap_hbm, snap, in_sem.at[0]),
        pltpu.make_async_copy(fi_hbm, fi, in_sem.at[1]),
        pltpu.make_async_copy(fo_hbm, fo, in_sem.at[2]),
        pltpu.make_async_copy(x0_hbm.at[pl.ds(pl.multiple_of(x * 1024, 1024), 1024)], x0, in_sem.at[3]),
    ]
    for load in loads:
        load.start()

    barrier = pltpu.get_barrier_semaphore()
    place = b * 4 + c

    def greet(i, carry):
        other = lax.rem(place + i, 32)
        pl.semaphore_signal(
            barrier, inc=1, device_id={"bin": other // 4, "row": x, "col": lax.rem(other, 4)}, device_id_type=MESH
        )
        return carry

    lax.fori_loop(1, 32, greet, 0)

    def greet_rows(i, carry):
        pl.semaphore_signal(
            barrier, inc=1, device_id={"bin": b, "row": lax.rem(x + 1 + i // 4, 4), "col": lax.rem(i, 4)},
            device_id_type=MESH,
        )
        return carry

    lax.fori_loop(0, 12, greet_rows, 0)

    loads[0].wait()
    loads[1].wait()
    for bb in range(8):
        proj[x, 16 * bb : 16 * bb + 16, :] = dot(snap[16 * bb : 16 * bb + 16, :], fi[bb], 1, 0)
    pl.semaphore_wait(barrier, 43)

    def row_exchange(buf, s, r):
        sends = []
        for i in (2, 1, 3):
            cp = rdma(buf.at[x], buf.at[x], s.at[i], r.at[i], at(mod4(x + i), y, z, k))
            cp.start()
            sends.append(cp)
        return sends

    def row_collect(buf, s, r):
        for i in (1, 3, 2):
            frm = mod4(x - i)
            rdma(buf.at[frm], buf.at[frm], s.at[i], r.at[i], at(frm, y, z, k)).wait_recv()
        return (buf[0] + buf[1]) + (buf[2] + buf[3])

    proj_sends = row_exchange(proj, p_s, p_r)
    loads[2].wait()
    projected = row_collect(proj, p_s, p_r).astype(BF16)
    here = z * 4 + y
    for bb in range(8):
        lifted = dot(projected[16 * bb : 16 * bb + 16, :], fo[bb], 1, 1)
        full[here, 16 * bb : 16 * bb + 16, :] = (
            snap[16 * bb : 16 * bb + 16, :].astype(F32) + lifted
        ).astype(BF16)

    is_source = zl == x // 2
    own_ci = lax.rem(x, 2)

    def slab_send(i):
        to = lax.rem(b + i, 8)
        return rdma(
            full.at[here, :, pl.ds(pl.multiple_of(to * 128, 128), 128)], slab.at[own_ci, here], a_s.at[i],
            a_r.at[here], {"bin": to, "row": x, "col": (x // 2) * 2 + k},
        )

    def start_slab(i, carry):
        slab_send(i).start()
        return carry

    lax.fori_loop(1, 8, start_slab, 0)
    slab_local = pltpu.make_async_copy(
        full.at[here, :, pl.ds(pl.multiple_of(b * 128, 128), 128)], slab.at[own_ci, here], l_sem.at[0]
    )

    @pl.when(is_source)
    def _():
        slab_local.start()

    @pl.when(jnp.logical_not(is_source))
    def _():
        slab_send(0).start()

    def block_of(half, u, v):
        return (v * 4 + u) if half == 0 else (u * 4 + v)

    def dev_of(half, u, v):
        return at(x, u, v, k) if half == 0 else at(x, v, u, k)

    def ring(half):
        return (y, z) if half == 0 else (z, y)

    def gcopy(half, event, u, v, lo, rows, tu, tv):
        blk = full.at[block_of(half, u, v), pl.ds(64 * half + lo, rows)]
        e = 20 * half + event
        return rdma(blk, blk, g_s.at[e], g_r.at[e], dev_of(half, tu, tv))

    pending = []

    def gsend(*args):
        cp = gcopy(*args)
        cp.start()
        pending.append(cp)

    def gwait(half, event, u, v, lo, rows):
        gcopy(half, event, u, v, lo, rows, mod4(ring(half)[0] + 1), v).wait_recv()

    def second_send(half, t):
        u, v = ring(half)
        w = mod4(u + (0, -1, 1, 2)[t])
        gsend(half, 4 + 4 * t, w, v, 0, 64, u, mod4(v + 1))
        gsend(half, 5 + 4 * t, w, v, 0, 64, u, mod4(v - 1))

    def second_forward(half, t):
        u, v = ring(half)
        w = mod4(u + (0, -1, 1, 2)[t])
        gwait(half, 4 + 4 * t, w, mod4(v - 1), 0, 64)
        gsend(half, 6 + 4 * t, w, mod4(v - 1), 0, 32, u, mod4(v + 1))
        gwait(half, 5 + 4 * t, w, mod4(v + 1), 0, 64)
        gsend(half, 7 + 4 * t, w, mod4(v + 1), 32, 32, u, mod4(v - 1))

    def second_last(half, t):
        u, v = ring(half)
        w = mod4(u + (0, -1, 1, 2)[t])
        gwait(half, 6 + 4 * t, w, mod4(v + 2), 0, 32)
        gwait(half, 7 + 4 * t, w, mod4(v + 2), 32, 32)

    for half in (0, 1):
        u, v = ring(half)
        gsend(half, 0, u, v, 0, 64, mod4(u + 1), v)
        gsend(half, 1, u, v, 0, 64, mod4(u - 1), v)
    for half in (0, 1):
        second_send(half, 0)
    for half in (0, 1):
        u, v = ring(half)
        gwait(half, 0, mod4(u - 1), v, 0, 64)
        gsend(half, 2, mod4(u - 1), v, 0, 32, mod4(u + 1), v)
        gwait(half, 1, mod4(u + 1), v, 0, 64)
        gsend(half, 3, mod4(u + 1), v, 32, 32, mod4(u - 1), v)
        second_send(half, 1)
        second_send(half, 2)

    def spread(ci, g, n, device):
        blk = slab.at[ci, pl.ds(4 * g, 4)]
        return rdma(blk, blk, x_s.at[ci, g, n], x_r.at[ci, g], device)

    right, left = at(mod4(x + 1), y, z, k), at(mod4(x - 1), y, z, k)

    @pl.when(is_source)
    def _():
        slab_local.wait()

        def arrived(i, carry):
            frm = lax.rem(here + i, 16)
            rdma(
                slab.at[own_ci, frm], slab.at[own_ci, frm], a_s.at[0], a_r.at[frm],
                at(x, lax.rem(frm, 4), frm // 4, k),
            ).wait_recv()
            return carry

        lax.fori_loop(1, 16, arrived, 0)
        for g in range(4):
            spread(own_ci, g, 0, right).start()
            spread(own_ci, g, 1, left).start()

    def spread_step(g):
        for ci in (0, 1):
            d = mod4(x - (2 * zl + ci))

            @pl.when(d != 0)
            def _():
                spread(ci, g, 0, right).wait_recv()

            @pl.when(d == (3 if ci == 0 else 1))
            def _():
                spread(ci, g, 0, left if ci == 0 else right).start()

    for half in (0, 1):
        second_forward(half, 0)
    for half in (0, 1):
        u, v = ring(half)
        gwait(half, 2, mod4(u + 2), v, 0, 32)
        gwait(half, 3, mod4(u + 2), v, 32, 32)
        second_send(half, 3)
    spread_step(0)
    for half in (0, 1):
        second_forward(half, 1)
        second_forward(half, 2)
    spread_step(1)
    spread_step(2)
    for half in (0, 1):
        second_forward(half, 3)
    spread_step(3)
    for half in (0, 1):
        for t in range(4):
            second_last(half, t)

    sib_sends = []
    lhs = jnp.concatenate([slab[0].reshape(2048, 128).T, slab[1].reshape(2048, 128).T], axis=0)
    for n in range(4):
        acc[n] = dot(lhs, full[:, :, 256 * n : 256 * n + 256].reshape(2048, 256), 1, 0)
        cp = rdma(
            acc.at[n, pl.ds(pl.multiple_of((1 - k) * 128, 128), 128)], sibc.at[n], c_s.at[n], c_r.at[n], sibling
        )
        cp.start()
        sib_sends.append(cp)
    scaling = 1.0 / 4096
    mine = pl.ds(pl.multiple_of(k * 128, 128), 128)
    for n in range(4):
        sib_sends[n].wait_recv()
        total = (acc[n, mine] + sibc[n]) * scaling
        piece[:, 256 * n : 256 * n + 256] = total
        cov_ref[b, :, 256 * n : 256 * n + 256] = total.astype(BF16)

    def csend(event, blk_b, lo, rows, device):
        blk = cov_ref.at[blk_b, pl.ds(lo, rows)]
        cp = rdma(blk, blk, v_s.at[event], v_r.at[event], device)
        cp.start()
        pending.append(cp)

    def cwait(event, blk_b, lo, rows):
        blk = cov_ref.at[blk_b, pl.ds(lo, rows)]
        rdma(blk, blk, v_s.at[event], v_r.at[event], sibling).wait_recv()

    yup, ydn = at(x, mod4(y + 1), z, k), at(x, mod4(y - 1), z, k)
    zfar = at(x, y, mod4(z + 2), k)
    yu, yd, yo = mod4(y + 1), mod4(y - 1), mod4(y + 2)
    far = 4 * (1 - zh)
    near = 4 * zh

    loads[3].wait()
    img[x] = dot(piece[...], x0[...], 1, 0, HI)
    img_sends = row_exchange(img, i_s, i_r)
    csend(2, b, 0, 128, zfar)
    csend(0, b, 0, 128, yup)
    csend(1, b, 0, 128, ydn)
    image = row_collect(img, i_s, i_r)

    gpart[...] = dot(image.T, image, 1, 0, HI)
    gsib_send = rdma(
        gpart.at[pl.ds(pl.multiple_of(32 * x + 16 * (1 - k), 16), 16)], gsib, gs_s.at[0], gs_r.at[0], sibling
    )
    gsib_send.start()

    part[...] = dot(piece[...].T, image, 1, 0, HI).reshape(2, 2, 256, 128)
    sibp_sends = []
    for h in (0, 1):
        cp = rdma(part.at[h, 1 - k], sibp.at[h], q_s.at[h], q_r.at[h], sibling)
        cp.start()
        sibp_sends.append(cp)

    gsib_send.wait_recv()
    gown[...] = gpart[pl.ds(pl.multiple_of(32 * x + 16 * k, 16), 16), :] + gsib[...]
    gscat[here] = gown[...]

    def plane_peer(i):
        other = lax.rem(here + i, 16)
        return at(x, lax.rem(other, 4), other // 4, k)

    def gram_send(i):
        return rdma(gown, gscat.at[here], ga_s.at[0, i], ga_r.at[0, i], plane_peer(i))

    def gram_start(i, carry):
        gram_send(i).start()
        return carry

    lax.fori_loop(1, 16, gram_start, 0)

    for h in (0, 1):
        sibp_sends[h].wait_recv()
        sibp[h] = sibp[h] + part[h, k]

    def scat_send(i):
        other = lax.rem(here + i, 16)
        oz = other // 4
        ob = (oz // 2) * 4 + lax.rem(other, 4)
        return rdma(
            sibp.at[lax.rem(oz, 2), pl.ds(pl.multiple_of(32 * ob, 32), 32)], scat.at[here], r_s.at[i], r_r.at[i],
            plane_peer(i),
        )

    def scat_start(i, carry):
        scat_send(i).start()
        return carry

    lax.fori_loop(1, 16, scat_start, 0)
    scat[here] = sibp[zl, pl.ds(pl.multiple_of(32 * b, 32), 32)]

    cwait(0, near + yd, 0, 128)
    csend(3, near + yd, 0, 64, yup)
    cwait(1, near + yu, 0, 128)
    csend(4, near + yu, 64, 64, ydn)

    def gram_arrived(i, carry):
        frm = lax.rem(here + 16 - i, 16)
        rdma(gown, gscat.at[frm], ga_s.at[0, i], ga_r.at[0, i], plane_peer(i)).wait_recv()
        return carry

    lax.fori_loop(1, 16, gram_arrived, 0)

    def add_slots(ref, n):
        total = ref[0]
        for i in range(1, n):
            total = total + ref[i]
        return total

    gslice = x * 2 + k
    gram[pl.ds(pl.multiple_of(16 * gslice, 16), 16), :] = add_slots(gscat, 16)

    def gram_share(buf, i, first):
        if first:
            own = gslice
            other = lax.rem(own + i, 8)
            device = at(other // 2, y, z, lax.rem(other, 2))
        else:
            own = b
            other = lax.rem(own + i, 8)
            device = {"bin": other, "row": x, "col": c}
        n = 0 if first else 1
        blk = buf.at[pl.ds(pl.multiple_of(16 * own, 16), 16)]
        return rdma(blk, blk, gb_s.at[n, i], gb_r.at[n, i], device)

    def share_wait(buf, i, first):
        own = gslice if first else b
        frm = lax.rem(own + 8 - i, 8)
        n = 0 if first else 1
        blk = buf.at[pl.ds(pl.multiple_of(16 * frm, 16), 16)]
        rdma(blk, blk, gb_s.at[n, i], gb_r.at[n, i], sibling).wait_recv()

    for i in range(1, 8):
        gram_share(gram, i, True).start()

    def scat_arrived(i, carry):
        frm = lax.rem(here + 16 - i, 16)
        rdma(scat.at[frm], scat.at[frm], r_s.at[i], r_r.at[i], plane_peer(i)).wait_recv()
        return carry

    lax.fori_loop(1, 16, scat_arrived, 0)
    zall[pl.ds(pl.multiple_of(32 * b, 32), 32), :] = add_slots(scat, 16)

    def bin_share(i):
        blk = zall.at[pl.ds(pl.multiple_of(32 * b, 32), 32)]
        return rdma(blk, blk, z_s.at[i], z_r.at[i], {"bin": lax.rem(b + i, 8), "row": x, "col": c})

    for i in range(1, 8):
        bin_share(i).start()

    cwait(2, far + y, 0, 128)
    csend(5, far + y, 0, 128, yup)
    csend(6, far + y, 0, 128, ydn)

    for i in range(1, 8):
        share_wait(gram, i, True)
    for i in range(1, 8):
        gram_share(gram, i, True).wait_send()
    invert_factor(gram)

    for i in range(1, 8):
        frm = lax.rem(b + 8 - i, 8)
        blk = zall.at[pl.ds(pl.multiple_of(32 * frm, 32), 32)]
        rdma(blk, blk, z_s.at[i], z_r.at[i], sibling).wait_recv()
    for i in range(1, 8):
        bin_share(i).wait_send()
    second = apply_factor(gram, zall[...])
    basis_ref[...] = second
    gpart2[...] = dot(second.T, second, 1, 0, HI)

    q = x * 4 + c
    gslice_rows = pl.ds(pl.multiple_of(16 * b, 16), 16)
    gscat2[q] = gpart2[gslice_rows, :]

    def mesh_peer(i):
        other = lax.rem(q + i, 16)
        return {"bin": b, "row": other // 4, "col": lax.rem(other, 4)}

    def gram2_send(i):
        oq = q
        return rdma(gscat2.at[oq], gscat2.at[oq], ga_s.at[1, i], ga_r.at[1, i], mesh_peer(i))

    def gram2_start(i, carry):
        gram2_send(i).start()
        return carry

    lax.fori_loop(1, 16, gram2_start, 0)

    cwait(5, far + yd, 0, 128)
    csend(7, far + yd, 0, 64, yup)
    cwait(6, far + yu, 0, 128)
    csend(8, far + yu, 64, 64, ydn)

    def gram2_arrived(i, carry):
        frm = lax.rem(q + 16 - i, 16)
        rdma(gscat2.at[frm], gscat2.at[frm], ga_s.at[1, i], ga_r.at[1, i], mesh_peer(i)).wait_recv()
        return carry

    lax.fori_loop(1, 16, gram2_arrived, 0)
    gram2[gslice_rows, :] = add_slots(gscat2, 16)
    for i in range(1, 8):
        gram_share(gram2, i, False).start()
    for i in range(1, 8):
        share_wait(gram2, i, False)
    for i in range(1, 8):
        gram_share(gram2, i, False).wait_send()
    invert_factor(gram2)
    basis_ref[...] = apply_factor(gram2, basis_ref[...]) * 64.0

    cwait(3, near + yo, 0, 64)
    cwait(4, near + yo, 64, 64)
    cwait(7, far + yo, 0, 64)
    cwait(8, far + yo, 64, 64)

    for cp in pending + proj_sends + img_sends + sib_sends + sibp_sends + [gsib_send]:
        cp.wait_send()

    def drain(i, carry):
        gram_send(i).wait_send()
        scat_send(i).wait_send()
        gram2_send(i).wait_send()
        return carry

    lax.fori_loop(1, 16, drain, 0)

    def drain_slab(i, carry):
        slab_send(i).wait_send()
        return carry

    lax.fori_loop(1, 8, drain_slab, 0)

    @pl.when(jnp.logical_not(is_source))
    def _():
        slab_send(0).wait_send()

    @pl.when(is_source)
    def _():
        for g in range(4):
            spread(own_ci, g, 0, right).wait_send()
            spread(own_ci, g, 1, left).wait_send()

    for ci in (0, 1):
        d = mod4(x - (2 * zl + ci))

        @pl.when(d == (3 if ci == 0 else 1))
        def _():
            for g in range(4):
                spread(ci, g, 0, left if ci == 0 else right).wait_send()


def shards(snapshots, focus_in, focus_out, start_basis):
    snaps = snapshots.transpose(1, 2, 0).reshape(128, 1024)
    dma = pltpu.SemaphoreType.DMA
    anywhere = pl.BlockSpec(memory_space=pl.ANY)
    in_vmem = pl.BlockSpec(memory_space=pltpu.VMEM)
    pieces, basis_out = pl.pallas_call(
        kernel,
        out_shape=(
            jax.ShapeDtypeStruct((8, 128, 1024), BF16),
            jax.ShapeDtypeStruct((256, 128), F32),
        ),
        in_specs=[anywhere] * 4,
        out_specs=(in_vmem, in_vmem),
        scratch_shapes=[
            pltpu.VMEM((128, 1024), BF16),
            pltpu.VMEM((8, 1024, 128), BF16),
            pltpu.VMEM((8, 1024, 128), BF16),
            pltpu.VMEM((1024, 128), F32),
            pltpu.VMEM((4, 128, 128), F32),
            pltpu.VMEM((16, 128, 1024), BF16),
            pltpu.VMEM((2, 16, 128, 128), BF16),
            pltpu.VMEM((4, 256, 256), F32),
            pltpu.VMEM((4, 128, 256), F32),
            pltpu.VMEM((128, 1024), F32),
            pltpu.VMEM((4, 128, 128), F32),
            pltpu.VMEM((2, 2, 256, 128), F32),
            pltpu.VMEM((2, 256, 128), F32),
            pltpu.VMEM((16, 32, 128), F32),
            pltpu.VMEM((256, 128), F32),
            pltpu.VMEM((128, 128), F32),
            pltpu.VMEM((16, 128), F32),
            pltpu.VMEM((16, 128), F32),
            pltpu.VMEM((16, 16, 128), F32),
            pltpu.VMEM((128, 128), F32),
            pltpu.VMEM((128, 128), F32),
            pltpu.VMEM((16, 16, 128), F32),
            pltpu.VMEM((128, 128), F32),
            dma((4,)),
            dma((4,)), dma((4,)),
            dma((40,)), dma((40,)),
            dma((8,)), dma((16,)),
            dma((2, 4, 2)), dma((2, 4)),
            dma((4,)), dma((4,)),
            dma((9,)), dma((9,)),
            dma((4,)), dma((4,)),
            dma((2,)), dma((2,)),
            dma((16,)), dma((16,)),
            dma((8,)), dma((8,)),
            dma((1,)), dma((1,)),
            dma((2, 16)), dma((2, 16)),
            dma((2, 8)), dma((2, 8)),
            dma((1,)),
        ],
        compiler_params=pltpu.CompilerParams(
            collective_id=0, has_side_effects=True, vmem_limit_bytes=40 * 2**20
        ),
    )(snaps, focus_in, focus_out, start_basis)
    return pieces.reshape(1024, 1024).astype(F32), basis_out


def solution(mesh):
    in_specs = (P("row", "bin", "col"), P("bin", "row", None), P("bin", "row", None), P())
    out_specs = (P("col", "row"), P(("row", "col"), None))
    return jax.shard_map(shards, mesh=mesh, in_specs=in_specs, out_specs=out_specs, check_vma=False)
```

time: 567 us -> 135 us (0.24); the launches traced: 559 us -> 135 us
  waiting for transfers between devices: 430 us -> 0 us
  Pallas kernels: 0 us -> 125 us
  other arithmetic: 48.4 us -> 2.61 us
  matrix products: 45.7 us -> 0 us
  blocking collectives: 14.6 us -> 0 us
  between operations: 14.7 us -> 0.65 us
    reduce_scatter x1 -> x0, waiting for transfers between devices: 185 us -> none  [shards(): lax.psum_scatter(lax.dot_general(permuted, local_rows, (((1,), (1,)), (()...]
    all_gather x4 -> x0, waiting for transfers between devices: 170 us -> none  [the longest x1 77.1 us: shards(): tile_block = lax.all_gather(share_rows, 'bin', axis=0, tiled=True)]
    pallas_call x0 -> x1, Pallas kernels: none -> 125 us  [shards(): pl.pallas_call(kernel, out_shape=(jax.ShapeDtypeStruct((8, 128, 1024), BF...]
    psum x2 -> x0, waiting for transfers between devices: 74.7 us -> none  [shards(): row_sums = lax.psum(partial_image, 'col')]
    another operation x10 -> x0, other arithmetic: 45.7 us -> none  [the longest x6 24.8 us: shards(): lower_factor = jnp.linalg.cholesky(gram_matrix)]
    dot_general x7 -> x0, matrix products: 38.5 us -> none  [the longest x2 16.3 us: shards(): lax.dot_general(covariance, col_rows, (((0,), (0,)), ((), ())), precision...]
    psum x1 -> x0, blocking collectives: 14.6 us -> none  [shards(): projected = lax.psum(partial_proj, 'row').astype(jnp.bfloat16)]
    another operation x2 -> x0, matrix products: 7.21 us -> none  [shards(): jax.scipy.linalg.solve_triangular(lower_factor, full_image.T, lower=True)]
  transfers between devices with their start and end apart: 7 -> 0, of which waited for: 7 -> 0; matrix products, arithmetic and copies ran while one was open for 0% -> 0% of each run, Pallas kernels for 0% -> 0%
where the time goes in v1:
time: 135 us
  Pallas kernels  125 us (93%)
  local copies, waits for them, and re-layouts  6.37 us (5%)
  other arithmetic  2.61 us (2%)
    pallas_call x1, Pallas kernels, shards(): pl.pallas_call(kernel, out_shape=(jax.ShapeDtypeStruct((8, 128, 1024), BF...  125 us
    unnamed x9, local copies, waits for them, and re-layouts  6.37 us

profile of v1, /device:TPU:1, one launch (start us, length us, event | category | flops | bytes accessed | tf_op | source)
XLA Modules:
  0.0 135.0 jit_solution(16055944618141983896)
XLA Ops:
  0.6 0.0 copy-start
  0.6 1.6 %copy-done = bf16[8,1024,128]{2,1,0:T(8,128)(2,1)S(1)} copy-done((bf16[8,1024,128]{2,1,0:T(8,128)(2,1)S(1)}, bf16[8,1024,128]{2,1,0:T(8,128)(2,1)}, u32[]{:S(2)}) %copy-start) | copy-done | bytes 2097176
  2.2 0.0 copy-start.1
  2.2 1.6 %copy-done.1 = bf16[8,1024,128]{2,1,0:T(8,128)(2,1)S(1)} copy-done((bf16[8,1024,128]{2,1,0:T(8,128)(2,1)S(1)}, bf16[8,1024,128]{2,1,0:T(8,128)(2,1)}, u32[]{:S(2)}) %copy-start.1) | copy-done | bytes 2097176
  3.8 0.0 copy-start.2
  3.8 1.6 %copy-done.2 = f32[4096,128]{1,0:T(8,128)S(1)} copy-done((f32[4096,128]{1,0:T(8,128)S(1)}, f32[4096,128]{1,0:T(8,128)}, u32[]{:S(2)}) %copy-start.2) | copy-done | bytes 2097176
  5.4 0.0 copy-start.3
  5.4 0.9 copy-done.3
  6.4 125.4 %shard_map.59 = (bf16[8,128,1024]{2,1,0:T(8,128)(2,1)S(1)}, f32[256,128]{1,0:T(8,128)S(1)}) custom-call(bf16[128,1024]{1,0:T(8,128)(2,1)S(1)} %bitcast.6, bf16[8,1024,128]{2,1,0:T(8,128)(2,1)S(1)} %copy-done, bf16[8,1024,128]{2,1,0:T(8,128)(2,1)S(1)} %copy-done.1, f32[4096,128]{1,0:T(8,128)S(1)} %copy-done.2), custom_call_target="tpu_custom_call" | custom-call | tf_op jit(solution)/shard_map/pallas_call | solution.py:534
  131.8 2.6 %bitcast_convert_fusion = f32[1024,1024]{1,0:T(8,128)} fusion(bf16[8,128,1024]{2,1,0:T(8,128)(2,1)S(1)} %get-tuple-element.4), kind=kLoop, calls=%fused_computation | loop fusion | flops 1048576 | bytes 6291456 | tf_op jit(solution)/shard_map/convert_element_type | solution.py:586
  134.4 0.7 copy.7
Async XLA Ops:
  0.6 1.6 %copy-start = (bf16[8,1024,128]{2,1,0:T(8,128)(2,1)S(1)}, bf16[8,1024,128]{2,1,0:T(8,128)(2,1)}, u32[]{:S(2)}) copy-start(bf16[8,1024,128]{2,1,0:T(8,128)(2,1)} %fi_hbm.1) | copy-start | bytes 6291460
  2.2 1.6 %copy-start.1 = (bf16[8,1024,128]{2,1,0:T(8,128)(2,1)S(1)}, bf16[8,1024,128]{2,1,0:T(8,128)(2,1)}, u32[]{:S(2)}) copy-start(bf16[8,1024,128]{2,1,0:T(8,128)(2,1)} %fo_hbm.1) | copy-start | bytes 6291460
  3.8 1.6 %copy-start.2 = (f32[4096,128]{1,0:T(8,128)S(1)}, f32[4096,128]{1,0:T(8,128)}, u32[]{:S(2)}) copy-start(f32[4096,128]{1,0:T(8,128)} %x0_hbm.1) | copy-start | bytes 6291460
  5.4 0.9 copy-start.3

commit v2 on v1

--- a/solution.py
+++ b/solution.py
@@ -22,31 +22,60 @@
     return lax.dot_general(a, b, (((ca,), (cb,)), ((), ())), precision=precision, preferred_element_type=F32)
 
 
-def invert_factor(work):
-    rows = lax.broadcasted_iota(jnp.int32, (128, 128), 0)
-    lanes = lax.broadcasted_iota(jnp.int32, (128, 128), 1)
-    lane1 = lax.broadcasted_iota(jnp.int32, (1, 128), 1)
-
-    def step(j, carry):
-        row = work[pl.ds(j, 1), :]
-        now = work[...]
-        col = jnp.sum(jnp.where(lanes == j, now, 0.0), axis=1, keepdims=True)
-        pivot = jnp.sum(jnp.where(lane1 == j, row, 0.0), axis=1, keepdims=True)
-        mult = jnp.where(rows > j, col / pivot, 0.0)
-        row = jnp.where(lane1 == j, 1.0, row)
-        work[...] = jnp.where((lanes == j) & (rows > j), 0.0, now) - mult * row
-        return carry
-
-    lax.fori_loop(0, 128, step, 0)
-
-
-def apply_factor(work, block):
-    rows = lax.broadcasted_iota(jnp.int32, (128, 128), 0)
-    lanes = lax.broadcasted_iota(jnp.int32, (128, 128), 1)
-    now = work[...]
-    pivots = jnp.sum(jnp.where(rows == lanes, now, 0.0), axis=0, keepdims=True)
-    inverse = jnp.where(rows > lanes, now, jnp.where(rows == lanes, 1.0, 0.0))
-    return dot(block, inverse, 1, 1, HI) * lax.rsqrt(pivots)
+def inverse_factor(gram):
+    lane = lax.broadcasted_iota(jnp.int32, (8, 128), 1)
+    sub = lax.broadcasted_iota(jnp.int32, (8, 128), 0)
+
+    def over_lanes(tile, j):
+        return jnp.broadcast_to(tile[:, j : j + 1], (8, 128))
+
+    def over_rows(tile, i):
+        return jnp.broadcast_to(tile[i : i + 1, :], (8, 128))
+
+    tiles = list(gram)
+    done = []
+    for p in range(16):
+        first = 8 * p
+        now = tiles[p]
+        cols = [over_lanes(now, first + e) for e in range(8)]
+        left = [[over_rows(cols[e], i) for e in range(i + 1)] for i in range(8)]
+        low = [[None] * 8 for _ in range(8)]
+        inv = [None] * 8
+        for e in range(8):
+            inv[e] = 1.0 / left[e][e]
+            for i in range(e + 1, 8):
+                low[i][e] = left[i][e] * inv[e]
+            for i in range(e + 1, 8):
+                for f in range(e + 1, i + 1):
+                    left[i][f] = left[i][f] - low[i][e] * left[f][e]
+        in_panel = (lane >= first) & (lane < first + 8)
+        upper = []
+        for i in range(8):
+            row = jnp.where(in_panel, jnp.where(lane == first + i, 1.0, 0.0), over_rows(now, i))
+            for e in range(i):
+                row = row - low[i][e] * upper[e]
+            upper.append(row)
+        tile, scale = upper[0], inv[0]
+        for i in range(1, 8):
+            tile = jnp.where(sub == i, upper[i], tile)
+            scale = jnp.where(sub == i, inv[i], scale)
+        done.append(jnp.where(lane <= sub + first, tile, 0.0) * jnp.sqrt(scale))
+        scaled = [upper[e] * inv[e] for e in range(8)]
+        for q in range(p + 1, 16):
+            total = jnp.where(in_panel, 0.0, tiles[q])
+            lower = []
+            for e in range(8):
+                col = over_lanes(tiles[q], first + e)
+                for f in range(e):
+                    col = col - lower[f] * low[e][f]
+                lower.append(col)
+                total = total - col * scaled[e]
+            tiles[q] = total
+    return jnp.concatenate(done, axis=0)
+
+
+def apply_factor(gram, block):
+    return dot(block, inverse_factor([gram[8 * i : 8 * i + 8, :] for i in range(16)]), 1, 1, HI)
 
 
 def kernel(
@@ -69,6 +98,7 @@
         return {"bin": (z_ // 2) * 4 + y_, "row": x_, "col": lax.rem(z_, 2) * 2 + k_}
 
     sibling = at(x, y, z, 1 - k)
+    pending, late = [], []
 
     def rdma(src, dst, s, r, device):
         return pltpu.make_async_remote_copy(
@@ -112,12 +142,10 @@
     pl.semaphore_wait(barrier, 43)
 
     def row_exchange(buf, s, r):
-        sends = []
         for i in (2, 1, 3):
             cp = rdma(buf.at[x], buf.at[x], s.at[i], r.at[i], at(mod4(x + i), y, z, k))
             cp.start()
-            sends.append(cp)
-        return sends
+            pending.append(cp)
 
     def row_collect(buf, s, r):
         for i in (1, 3, 2):
@@ -125,7 +153,14 @@
             rdma(buf.at[frm], buf.at[frm], s.at[i], r.at[i], at(frm, y, z, k)).wait_recv()
         return (buf[0] + buf[1]) + (buf[2] + buf[3])
 
-    proj_sends = row_exchange(proj, p_s, p_r)
+    row_exchange(proj, p_s, p_r)
+    def loop_wait(send, n):
+        def one(i, carry):
+            send(i).wait_send()
+            return carry
+
+        late.append(lambda: lax.fori_loop(1, n, one, 0))
+
     loads[2].wait()
     projected = row_collect(proj, p_s, p_r).astype(BF16)
     here = z * 4 + y
@@ -150,6 +185,7 @@
         return carry
 
     lax.fori_loop(1, 8, start_slab, 0)
+    loop_wait(slab_send, 8)
     slab_local = pltpu.make_async_copy(
         full.at[here, :, pl.ds(pl.multiple_of(b * 128, 128), 128)], slab.at[own_ci, here], l_sem.at[0]
     )
@@ -161,6 +197,13 @@
     @pl.when(jnp.logical_not(is_source))
     def _():
         slab_send(0).start()
+
+    def finish_slab():
+        @pl.when(jnp.logical_not(is_source))
+        def _():
+            slab_send(0).wait_send()
+
+    late.append(finish_slab)
 
     def block_of(half, u, v):
         return (v * 4 + u) if half == 0 else (u * 4 + v)
@@ -175,8 +218,6 @@
         blk = full.at[block_of(half, u, v), pl.ds(64 * half + lo, rows)]
         e = 20 * half + event
         return rdma(blk, blk, g_s.at[e], g_r.at[e], dev_of(half, tu, tv))
-
-    pending = []
 
     def gsend(*args):
         cp = gcopy(*args)
@@ -255,6 +296,23 @@
             @pl.when(d == (3 if ci == 0 else 1))
             def _():
                 spread(ci, g, 0, left if ci == 0 else right).start()
+
+    def finish_spread():
+        @pl.when(is_source)
+        def _():
+            for g in range(4):
+                spread(own_ci, g, 0, right).wait_send()
+                spread(own_ci, g, 1, left).wait_send()
+
+        for ci in (0, 1):
+            d = mod4(x - (2 * zl + ci))
+
+            @pl.when(d == (3 if ci == 0 else 1))
+            def _():
+                for g in range(4):
+                    spread(ci, g, 0, left if ci == 0 else right).wait_send()
+
+    late.append(finish_spread)
 
     for half in (0, 1):
         second_forward(half, 0)
@@ -285,6 +343,7 @@
         )
         cp.start()
         sib_sends.append(cp)
+        pending.append(cp)
     scaling = 1.0 / 4096
     mine = pl.ds(pl.multiple_of(k * 128, 128), 128)
     for n in range(4):
@@ -311,7 +370,7 @@
 
     loads[3].wait()
     img[x] = dot(piece[...], x0[...], 1, 0, HI)
-    img_sends = row_exchange(img, i_s, i_r)
+    row_exchange(img, i_s, i_r)
     csend(2, b, 0, 128, zfar)
     csend(0, b, 0, 128, yup)
     csend(1, b, 0, 128, ydn)
@@ -322,6 +381,7 @@
         gpart.at[pl.ds(pl.multiple_of(32 * x + 16 * (1 - k), 16), 16)], gsib, gs_s.at[0], gs_r.at[0], sibling
     )
     gsib_send.start()
+    pending.append(gsib_send)
 
     part[...] = dot(piece[...].T, image, 1, 0, HI).reshape(2, 2, 256, 128)
     sibp_sends = []
@@ -329,6 +389,7 @@
         cp = rdma(part.at[h, 1 - k], sibp.at[h], q_s.at[h], q_r.at[h], sibling)
         cp.start()
         sibp_sends.append(cp)
+        pending.append(cp)
 
     gsib_send.wait_recv()
     gown[...] = gpart[pl.ds(pl.multiple_of(32 * x + 16 * k, 16), 16), :] + gsib[...]
@@ -346,6 +407,7 @@
         return carry
 
     lax.fori_loop(1, 16, gram_start, 0)
+    loop_wait(gram_send, 16)
 
     for h in (0, 1):
         sibp_sends[h].wait_recv()
@@ -365,6 +427,7 @@
         return carry
 
     lax.fori_loop(1, 16, scat_start, 0)
+    loop_wait(scat_send, 16)
     scat[here] = sibp[zl, pl.ds(pl.multiple_of(32 * b, 32), 32)]
 
     cwait(0, near + yd, 0, 128)
@@ -410,6 +473,7 @@
 
     for i in range(1, 8):
         gram_share(gram, i, True).start()
+        pending.append(gram_share(gram, i, True))
 
     def scat_arrived(i, carry):
         frm = lax.rem(here + 16 - i, 16)
@@ -425,6 +489,7 @@
 
     for i in range(1, 8):
         bin_share(i).start()
+        pending.append(bin_share(i))
 
     cwait(2, far + y, 0, 128)
     csend(5, far + y, 0, 128, yup)
@@ -432,17 +497,12 @@
 
     for i in range(1, 8):
         share_wait(gram, i, True)
-    for i in range(1, 8):
-        gram_share(gram, i, True).wait_send()
-    invert_factor(gram)
-
+    inverse = inverse_factor([gram[8 * i : 8 * i + 8, :] for i in range(16)])
     for i in range(1, 8):
         frm = lax.rem(b + 8 - i, 8)
         blk = zall.at[pl.ds(pl.multiple_of(32 * frm, 32), 32)]
         rdma(blk, blk, z_s.at[i], z_r.at[i], sibling).wait_recv()
-    for i in range(1, 8):
-        bin_share(i).wait_send()
-    second = apply_factor(gram, zall[...])
+    second = dot(zall[...], inverse, 1, 1, HI)
     basis_ref[...] = second
     gpart2[...] = dot(second.T, second, 1, 0, HI)
 
@@ -463,6 +523,7 @@
         return carry
 
     lax.fori_loop(1, 16, gram2_start, 0)
+    loop_wait(gram2_send, 16)
 
     cwait(5, far + yd, 0, 128)
     csend(7, far + yd, 0, 64, yup)
@@ -478,11 +539,9 @@
     gram2[gslice_rows, :] = add_slots(gscat2, 16)
     for i in range(1, 8):
         gram_share(gram2, i, False).start()
+        pending.append(gram_share(gram2, i, False))
     for i in range(1, 8):
         share_wait(gram2, i, False)
-    for i in range(1, 8):
-        gram_share(gram2, i, False).wait_send()
-    invert_factor(gram2)
     basis_ref[...] = apply_factor(gram2, basis_ref[...]) * 64.0
 
     cwait(3, near + yo, 0, 64)
@@ -490,40 +549,10 @@
     cwait(7, far + yo, 0, 64)
     cwait(8, far + yo, 64, 64)
 
-    for cp in pending + proj_sends + img_sends + sib_sends + sibp_sends + [gsib_send]:
+    for cp in pending:
         cp.wait_send()
-
-    def drain(i, carry):
-        gram_send(i).wait_send()
-        scat_send(i).wait_send()
-        gram2_send(i).wait_send()
-        return carry
-
-    lax.fori_loop(1, 16, drain, 0)
-
-    def drain_slab(i, carry):
-        slab_send(i).wait_send()
-        return carry
-
-    lax.fori_loop(1, 8, drain_slab, 0)
-
-    @pl.when(jnp.logical_not(is_source))
-    def _():
-        slab_send(0).wait_send()
-
-    @pl.when(is_source)
-    def _():
-        for g in range(4):
-            spread(own_ci, g, 0, right).wait_send()
-            spread(own_ci, g, 1, left).wait_send()
-
-    for ci in (0, 1):
-        d = mod4(x - (2 * zl + ci))
-
-        @pl.when(d == (3 if ci == 0 else 1))
-        def _():
-            for g in range(4):
-                spread(ci, g, 0, left if ci == 0 else right).wait_send()
+    for finish in late:
+        finish()
 
 
 def shards(snapshots, focus_in, focus_out, start_basis):

time: 135 us -> 119 us (0.88)
  Pallas kernels: 125 us -> 109 us
    pallas_call x1, Pallas kernels: 125 us -> 109 us  [shards(): pl.pallas_call(kernel, out_shape=(jax.ShapeDtypeStruct((8, 128, 1024), BF...]
where the time goes in v2:
time: 119 us
  Pallas kernels  109 us (92%)
  local copies, waits for them, and re-layouts  6.37 us (5%)
  other arithmetic  2.61 us (2%)
    pallas_call x1, Pallas kernels, shards(): pl.pallas_call(kernel, out_shape=(jax.ShapeDtypeStruct((8, 128, 1024), BF...  109 us
    unnamed x9, local copies, waits for them, and re-layouts  6.37 us
    convert_element_type x1, other arithmetic, shards(): return (pieces.reshape(1024, 1024).astype(F32), basis_out)  2.61 us

profile of v2, /device:TPU:1, one launch (start us, length us, event | category | flops | bytes accessed | tf_op | source)
XLA Modules:
  0.0 119.0 jit_solution(16887371931749512080)
XLA Ops:
  0.6 0.0 copy-start
  0.6 1.6 %copy-done = bf16[8,1024,128]{2,1,0:T(8,128)(2,1)S(1)} copy-done((bf16[8,1024,128]{2,1,0:T(8,128)(2,1)S(1)}, bf16[8,1024,128]{2,1,0:T(8,128)(2,1)}, u32[]{:S(2)}) %copy-start) | copy-done | bytes 2097176
  2.2 0.0 copy-start.1
  2.2 1.6 %copy-done.1 = bf16[8,1024,128]{2,1,0:T(8,128)(2,1)S(1)} copy-done((bf16[8,1024,128]{2,1,0:T(8,128)(2,1)S(1)}, bf16[8,1024,128]{2,1,0:T(8,128)(2,1)}, u32[]{:S(2)}) %copy-start.1) | copy-done | bytes 2097176
  3.8 0.0 copy-start.2
  3.8 1.6 %copy-done.2 = f32[4096,128]{1,0:T(8,128)S(1)} copy-done((f32[4096,128]{1,0:T(8,128)S(1)}, f32[4096,128]{1,0:T(8,128)}, u32[]{:S(2)}) %copy-start.2) | copy-done | bytes 2097176
  5.4 0.0 copy-start.3
  5.4 0.9 copy-done.3
  6.4 109.4 %shard_map.59 = (bf16[8,128,1024]{2,1,0:T(8,128)(2,1)S(1)}, f32[256,128]{1,0:T(8,128)S(1)}) custom-call(bf16[128,1024]{1,0:T(8,128)(2,1)S(1)} %bitcast.6, bf16[8,1024,128]{2,1,0:T(8,128)(2,1)S(1)} %copy-done, bf16[8,1024,128]{2,1,0:T(8,128)(2,1)S(1)} %copy-done.1, f32[4096,128]{1,0:T(8,128)S(1)} %copy-done.2), custom_call_target="tpu_custom_call" | custom-call | tf_op jit(solution)/shard_map/pallas_call | solution.py:563
  115.7 2.6 %bitcast_convert_fusion = f32[1024,1024]{1,0:T(8,128)} fusion(bf16[8,128,1024]{2,1,0:T(8,128)(2,1)S(1)} %get-tuple-element.4), kind=kLoop, calls=%fused_computation | loop fusion | flops 1048576 | bytes 6291456 | tf_op jit(solution)/shard_map/convert_element_type | solution.py:615
  118.3 0.7 copy.7
Async XLA Ops:
  0.6 1.6 %copy-start = (bf16[8,1024,128]{2,1,0:T(8,128)(2,1)S(1)}, bf16[8,1024,128]{2,1,0:T(8,128)(2,1)}, u32[]{:S(2)}) copy-start(bf16[8,1024,128]{2,1,0:T(8,128)(2,1)} %fi_hbm.1) | copy-start | bytes 6291460
  2.2 1.6 %copy-start.1 = (bf16[8,1024,128]{2,1,0:T(8,128)(2,1)S(1)}, bf16[8,1024,128]{2,1,0:T(8,128)(2,1)}, u32[]{:S(2)}) copy-start(bf16[8,1024,128]{2,1,0:T(8,128)(2,1)} %fo_hbm.1) | copy-start | bytes 6291460
  3.8 1.6 %copy-start.2 = (f32[4096,128]{1,0:T(8,128)S(1)}, f32[4096,128]{1,0:T(8,128)}, u32[]{:S(2)}) copy-start(f32[4096,128]{1,0:T(8,128)} %x0_hbm.1) | copy-start | bytes 6291460
  5.4 0.9 copy-start.3

commit v3 on v2

--- a/solution.py
+++ b/solution.py
@@ -285,17 +285,27 @@
             spread(own_ci, g, 0, right).start()
             spread(own_ci, g, 1, left).start()
 
-    def spread_step(g):
+    def spread_roles(forward):
         for ci in (0, 1):
             d = mod4(x - (2 * zl + ci))
-
-            @pl.when(d != 0)
+            passes_on = d == (3 if ci == 0 else 1)
+            yield ci, (passes_on if forward else (d != 0) & jnp.logical_not(passes_on))
+
+    def spread_step(g):
+        for ci, passes_on in spread_roles(True):
+
+            @pl.when(passes_on)
             def _():
                 spread(ci, g, 0, right).wait_recv()
-
-            @pl.when(d == (3 if ci == 0 else 1))
+                spread(ci, g, 0, left if ci == 0 else right).start()
+
+    def spread_last():
+        for ci, receives in spread_roles(False):
+
+            @pl.when(receives)
             def _():
-                spread(ci, g, 0, left if ci == 0 else right).start()
+                for g in range(4):
+                    spread(ci, g, 0, right).wait_recv()
 
     def finish_spread():
         @pl.when(is_source)
@@ -304,10 +314,9 @@
                 spread(own_ci, g, 0, right).wait_send()
                 spread(own_ci, g, 1, left).wait_send()
 
-        for ci in (0, 1):
-            d = mod4(x - (2 * zl + ci))
-
-            @pl.when(d == (3 if ci == 0 else 1))
+        for ci, passes_on in spread_roles(True):
+
+            @pl.when(passes_on)
             def _():
                 for g in range(4):
                     spread(ci, g, 0, left if ci == 0 else right).wait_send()
@@ -333,6 +342,8 @@
     for half in (0, 1):
         for t in range(4):
             second_last(half, t)
+
+    spread_last()
 
     sib_sends = []
     lhs = jnp.concatenate([slab[0].reshape(2048, 128).T, slab[1].reshape(2048, 128).T], axis=0)
@@ -566,7 +577,7 @@
             jax.ShapeDtypeStruct((8, 128, 1024), BF16),
             jax.ShapeDtypeStruct((256, 128), F32),
         ),
-        in_specs=[anywhere] * 4,
+        in_specs=[pl.BlockSpec(memory_space=pltpu.HBM)] * 4,
         out_specs=(in_vmem, in_vmem),
         scratch_shapes=[
             pltpu.VMEM((128, 1024), BF16),
@@ -609,7 +620,7 @@
             dma((1,)),
         ],
         compiler_params=pltpu.CompilerParams(
-            collective_id=0, has_side_effects=True, vmem_limit_bytes=40 * 2**20
+            collective_id=0, has_side_effects=True, vmem_limit_bytes=60 * 2**20
         ),
     )(snaps, focus_in, focus_out, start_basis)
     return pieces.reshape(1024, 1024).astype(F32), basis_out

time: 119 us -> 94.8 us (0.80)
  Pallas kernels: 109 us -> 89.2 us
  local copies, waits for them, and re-layouts: 6.37 us -> 0.66 us
  other arithmetic: 2.61 us -> 4.1 us
    pallas_call x1, Pallas kernels: 109 us -> 89.2 us  [shards(): pl.pallas_call(kernel, out_shape=(jax.ShapeDtypeStruct((8, 128, 1024), BF...]
    unnamed x9 -> x3, local copies, waits for them, and re-layouts: 6.37 us -> 0.66 us
    convert_element_type x1, other arithmetic: 2.61 us -> 4.1 us  [shards(): return (pieces.reshape(1024, 1024).astype(F32), basis_out)]
where the time goes in v3:
time: 94.8 us; the launch traced here: 94.6 us
  Pallas kernels  89.2 us (94%)
  other arithmetic  4.1 us (4%)
    pallas_call x1, Pallas kernels, shards(): pl.pallas_call(kernel, out_shape=(jax.ShapeDtypeStruct((8, 128, 1024), BF...  89.2 us
    convert_element_type x1, other arithmetic, shards(): return (pieces.reshape(1024, 1024).astype(F32), basis_out)  4.1 us

profile of v3, /device:TPU:1, one launch (start us, length us, event | category | flops | bytes accessed | tf_op | source)
XLA Modules:
  0.0 94.6 jit_solution(3839079507005471456)
XLA Ops:
  0.6 89.2 %shard_map.59 = (bf16[8,128,1024]{2,1,0:T(8,128)(2,1)}, f32[256,128]{1,0:T(8,128)}) custom-call(bf16[128,1024]{1,0:T(8,128)(2,1)} %bitcast.6, bf16[8,1024,128]{2,1,0:T(8,128)(2,1)} %fi_hbm.1, bf16[8,1024,128]{2,1,0:T(8,128)(2,1)} %fo_hbm.1, f32[4096,128]{1,0:T(8,128)} %x0_hbm.1), custom_call_target="tpu_custom_call" | custom-call | tf_op jit(solution)/shard_map/pallas_call | solution.py:574
  89.9 0.0 copy-start
  89.9 4.1 %bitcast_convert_fusion = f32[1024,1024]{1,0:T(8,128)} fusion(bf16[8,128,1024]{2,1,0:T(8,128)(2,1)} %get-tuple-element.4), kind=kLoop, calls=%fused_computation | loop fusion | flops 1048576 | bytes 6291456 | tf_op jit(solution)/shard_map/convert_element_type | solution.py:626
  94.0 0.0 copy-done
  94.0 0.7 copy.7
Async XLA Ops:
  89.9 4.1 %copy-start = (f32[256,128]{1,0:T(8,128)S(1)}, f32[256,128]{1,0:T(8,128)}, u32[]{:S(2)}) copy-start(f32[256,128]{1,0:T(8,128)} %get-tuple-element.9) | copy-start | bytes 393220

commit v4 on v3

--- a/solution.py
+++ b/solution.py
@@ -20,6 +20,12 @@
 
 def dot(a, b, ca, cb, precision=None):
     return lax.dot_general(a, b, (((ca,), (cb,)), ((), ())), precision=precision, preferred_element_type=F32)
+
+
+def dot_split(a, b, ca, cb):
+    high = b.astype(BF16)
+    low = (b - high.astype(F32)).astype(BF16)
+    return dot(a, high, ca, cb) + dot(a, low, ca, cb)
 
 
 def inverse_factor(gram):
@@ -80,10 +86,10 @@
 
 def kernel(
     snap_hbm, fi_hbm, fo_hbm, x0_hbm, cov_ref, basis_ref,
-    snap, fi, fo, x0, proj, full, slab, acc, sibc, piece, img, part, sibp, scat, zall,
+    snap, fi, fo, x0, proj, full, slab, acc, sibc, piece, img, part, sibp, scat, zall, xr, img2, image2, last,
     gpart, gsib, gown, gscat, gram, gpart2, gscat2, gram2, in_sem,
     p_s, p_r, g_s, g_r, a_s, a_r, x_s, x_r, c_s, c_r, v_s, v_r, i_s, i_r, q_s, q_r, r_s, r_r, z_s, z_r,
-    gs_s, gs_r, ga_s, ga_r, gb_s, gb_r, l_sem,
+    y_s, y_r, j_s, j_r, o_s, o_r, gs_s, gs_r, ga_s, ga_r, gb_s, gb_r, l_sem,
 ):
     b = lax.axis_index("bin")
     x = lax.axis_index("row")
@@ -253,6 +259,11 @@
         gsend(half, 1, u, v, 0, 64, mod4(u - 1), v)
     for half in (0, 1):
         second_send(half, 0)
+
+    loads[3].wait()
+    img[x] = dot_split(full[here], x0[...], 1, 0)
+    row_exchange(img, i_s, i_r)
+
     for half in (0, 1):
         u, v = ring(half)
         gwait(half, 0, mod4(u - 1), v, 0, 64)
@@ -262,6 +273,15 @@
         second_send(half, 1)
         second_send(half, 2)
 
+    weights = row_collect(img, i_s, i_r)
+    part[...] = (dot_split(full[here].T, weights, 1, 0) * (1.0 / 4096)).reshape(2, 2, 256, 128)
+    sibp_sends = []
+    for h in (0, 1):
+        cp = rdma(part.at[h, 1 - k], sibp.at[h], q_s.at[h], q_r.at[h], sibling)
+        cp.start()
+        sibp_sends.append(cp)
+        pending.append(cp)
+
     def spread(ci, g, n, device):
         blk = slab.at[ci, pl.ds(4 * g, 4)]
         return rdma(blk, blk, x_s.at[ci, g, n], x_r.at[ci, g], device)
@@ -325,100 +345,16 @@
 
     for half in (0, 1):
         second_forward(half, 0)
-    for half in (0, 1):
-        u, v = ring(half)
-        gwait(half, 2, mod4(u + 2), v, 0, 32)
-        gwait(half, 3, mod4(u + 2), v, 32, 32)
-        second_send(half, 3)
-    spread_step(0)
-    for half in (0, 1):
-        second_forward(half, 1)
-        second_forward(half, 2)
-    spread_step(1)
-    spread_step(2)
-    for half in (0, 1):
-        second_forward(half, 3)
-    spread_step(3)
-    for half in (0, 1):
-        for t in range(4):
-            second_last(half, t)
-
-    spread_last()
-
-    sib_sends = []
-    lhs = jnp.concatenate([slab[0].reshape(2048, 128).T, slab[1].reshape(2048, 128).T], axis=0)
-    for n in range(4):
-        acc[n] = dot(lhs, full[:, :, 256 * n : 256 * n + 256].reshape(2048, 256), 1, 0)
-        cp = rdma(
-            acc.at[n, pl.ds(pl.multiple_of((1 - k) * 128, 128), 128)], sibc.at[n], c_s.at[n], c_r.at[n], sibling
-        )
-        cp.start()
-        sib_sends.append(cp)
-        pending.append(cp)
-    scaling = 1.0 / 4096
-    mine = pl.ds(pl.multiple_of(k * 128, 128), 128)
-    for n in range(4):
-        sib_sends[n].wait_recv()
-        total = (acc[n, mine] + sibc[n]) * scaling
-        piece[:, 256 * n : 256 * n + 256] = total
-        cov_ref[b, :, 256 * n : 256 * n + 256] = total.astype(BF16)
-
-    def csend(event, blk_b, lo, rows, device):
-        blk = cov_ref.at[blk_b, pl.ds(lo, rows)]
-        cp = rdma(blk, blk, v_s.at[event], v_r.at[event], device)
-        cp.start()
-        pending.append(cp)
-
-    def cwait(event, blk_b, lo, rows):
-        blk = cov_ref.at[blk_b, pl.ds(lo, rows)]
-        rdma(blk, blk, v_s.at[event], v_r.at[event], sibling).wait_recv()
-
-    yup, ydn = at(x, mod4(y + 1), z, k), at(x, mod4(y - 1), z, k)
-    zfar = at(x, y, mod4(z + 2), k)
-    yu, yd, yo = mod4(y + 1), mod4(y - 1), mod4(y + 2)
-    far = 4 * (1 - zh)
-    near = 4 * zh
-
-    loads[3].wait()
-    img[x] = dot(piece[...], x0[...], 1, 0, HI)
-    row_exchange(img, i_s, i_r)
-    csend(2, b, 0, 128, zfar)
-    csend(0, b, 0, 128, yup)
-    csend(1, b, 0, 128, ydn)
-    image = row_collect(img, i_s, i_r)
-
-    gpart[...] = dot(image.T, image, 1, 0, HI)
-    gsib_send = rdma(
-        gpart.at[pl.ds(pl.multiple_of(32 * x + 16 * (1 - k), 16), 16)], gsib, gs_s.at[0], gs_r.at[0], sibling
-    )
-    gsib_send.start()
-    pending.append(gsib_send)
-
-    part[...] = dot(piece[...].T, image, 1, 0, HI).reshape(2, 2, 256, 128)
-    sibp_sends = []
-    for h in (0, 1):
-        cp = rdma(part.at[h, 1 - k], sibp.at[h], q_s.at[h], q_r.at[h], sibling)
-        cp.start()
-        sibp_sends.append(cp)
-        pending.append(cp)
-
-    gsib_send.wait_recv()
-    gown[...] = gpart[pl.ds(pl.multiple_of(32 * x + 16 * k, 16), 16), :] + gsib[...]
-    gscat[here] = gown[...]
 
     def plane_peer(i):
         other = lax.rem(here + i, 16)
         return at(x, lax.rem(other, 4), other // 4, k)
 
-    def gram_send(i):
-        return rdma(gown, gscat.at[here], ga_s.at[0, i], ga_r.at[0, i], plane_peer(i))
-
-    def gram_start(i, carry):
-        gram_send(i).start()
-        return carry
-
-    lax.fori_loop(1, 16, gram_start, 0)
-    loop_wait(gram_send, 16)
+    def add_slots(ref, n):
+        total = ref[0]
+        for i in range(1, n):
+            total = total + ref[i]
+        return total
 
     for h in (0, 1):
         sibp_sends[h].wait_recv()
@@ -441,119 +377,265 @@
     loop_wait(scat_send, 16)
     scat[here] = sibp[zl, pl.ds(pl.multiple_of(32 * b, 32), 32)]
 
+    for half in (0, 1):
+        u, v = ring(half)
+        gwait(half, 2, mod4(u + 2), v, 0, 32)
+        gwait(half, 3, mod4(u + 2), v, 32, 32)
+        second_send(half, 3)
+    spread_step(0)
+    for half in (0, 1):
+        second_forward(half, 1)
+
+    def scat_arrived(i, carry):
+        frm = lax.rem(here + 16 - i, 16)
+        rdma(scat.at[frm], scat.at[frm], r_s.at[i], r_r.at[i], plane_peer(i)).wait_recv()
+        return carry
+
+    lax.fori_loop(1, 16, scat_arrived, 0)
+    zall[pl.ds(pl.multiple_of(32 * b, 32), 32), :] = add_slots(scat, 16)
+
+    def bin_share(i):
+        blk = zall.at[pl.ds(pl.multiple_of(32 * b, 32), 32)]
+        return rdma(blk, blk, z_s.at[i], z_r.at[i], {"bin": lax.rem(b + i, 8), "row": x, "col": c})
+
+    for i in range(1, 8):
+        bin_share(i).start()
+        pending.append(bin_share(i))
+
+    for half in (0, 1):
+        second_forward(half, 2)
+    spread_step(1)
+    spread_step(2)
+
+    for i in range(1, 8):
+        frm = lax.rem(b + 8 - i, 8)
+        blk = zall.at[pl.ds(pl.multiple_of(32 * frm, 32), 32)]
+        rdma(blk, blk, z_s.at[i], z_r.at[i], sibling).wait_recv()
+
+    def col_share(i):
+        return rdma(zall, xr.at[c], y_s.at[i], y_r.at[i], {"bin": b, "row": x, "col": mod4(c + i)})
+
+    for i in (2, 1, 3):
+        col_share(i).start()
+        pending.append(col_share(i))
+    first = zall[...]
+    xr[c] = first
+    gpart[...] = dot(first.T, first, 1, 0, HI)
+    q = x * 4 + c
+    bin_slice = pl.ds(pl.multiple_of(16 * b, 16), 16)
+    gscat2[q] = gpart[bin_slice, :]
+
+    def mesh_peer(i):
+        other = lax.rem(q + i, 16)
+        return {"bin": b, "row": other // 4, "col": lax.rem(other, 4)}
+
+    def gram_send(i):
+        return rdma(gscat2.at[q], gscat2.at[q], ga_s.at[0, i], ga_r.at[0, i], mesh_peer(i))
+
+    def gram_start(i, carry):
+        gram_send(i).start()
+        return carry
+
+    lax.fori_loop(1, 16, gram_start, 0)
+    loop_wait(gram_send, 16)
+
+    for half in (0, 1):
+        second_forward(half, 3)
+    spread_step(3)
+
+    def gram_share(buf, i, n):
+        if n == 0:
+            own = b
+            other = lax.rem(own + i, 8)
+            device = {"bin": other, "row": x, "col": c}
+        else:
+            own = x * 2 + k
+            other = lax.rem(own + i, 8)
+            device = at(other // 2, y, z, lax.rem(other, 2))
+        blk = buf.at[pl.ds(pl.multiple_of(16 * own, 16), 16)]
+        return rdma(blk, blk, gb_s.at[n, i], gb_r.at[n, i], device)
+
+    def share_start(buf, n):
+        for i in range(1, 8):
+            gram_share(buf, i, n).start()
+            pending.append(gram_share(buf, i, n))
+
+    def share_wait(buf, n):
+        own = b if n == 0 else x * 2 + k
+        for i in range(1, 8):
+            frm = lax.rem(own + 8 - i, 8)
+            blk = buf.at[pl.ds(pl.multiple_of(16 * frm, 16), 16)]
+            rdma(blk, blk, gb_s.at[n, i], gb_r.at[n, i], sibling).wait_recv()
+
+    def gram_arrived(i, carry):
+        frm = lax.rem(q + 16 - i, 16)
+        rdma(gscat2.at[frm], gscat2.at[frm], ga_s.at[0, i], ga_r.at[0, i], mesh_peer(i)).wait_recv()
+        return carry
+
+    lax.fori_loop(1, 16, gram_arrived, 0)
+    gram[bin_slice, :] = add_slots(gscat2, 16)
+    share_start(gram, 0)
+    spread_last()
+
+    def stack(places):
+        lhs = [
+            jnp.concatenate([slab[ci, j, 64 * half : 64 * half + 64, :] for half, j in places], axis=0).T
+            for ci in (0, 1)
+        ]
+        return jnp.concatenate(lhs, axis=0)
+
+    def multiply(places, lhs, n):
+        rhs = jnp.concatenate(
+            [full[j, 64 * half : 64 * half + 64, 256 * n : 256 * n + 256] for half, j in places], axis=0
+        )
+        return dot(lhs, rhs, 1, 0)
+
+    early, late_blocks = [], []
+    for half in (0, 1):
+        u, v = ring(half)
+        for i in (0, 1, 3, 2):
+            for w in range(4):
+                (late_blocks if i == 2 else early).append((half, block_of(half, w, mod4(v + i))))
+    lhs = stack(early)
+    for n in range(4):
+        acc[n] = multiply(early, lhs, n)
+    for half in (0, 1):
+        for t in range(4):
+            second_last(half, t)
+    sib_sends = []
+    lhs = stack(late_blocks)
+    for n in range(4):
+        acc[n] = acc[n] + multiply(late_blocks, lhs, n)
+        cp = rdma(
+            acc.at[n, pl.ds(pl.multiple_of((1 - k) * 128, 128), 128)], sibc.at[n], c_s.at[n], c_r.at[n], sibling
+        )
+        cp.start()
+        sib_sends.append(cp)
+        pending.append(cp)
+    for i in (1, 2, 3):
+        frm = mod4(c - i)
+        rdma(zall, xr.at[frm], y_s.at[i], y_r.at[i], sibling).wait_recv()
+    scaling = 1.0 / 4096
+    mine = pl.ds(pl.multiple_of(k * 128, 128), 128)
+    for n in range(4):
+        sib_sends[n].wait_recv()
+        total = (acc[n, mine] + sibc[n]) * scaling
+        piece[:, 256 * n : 256 * n + 256] = total
+        cov_ref[b, :, 256 * n : 256 * n + 256] = total.astype(BF16)
+
+    img2[x] = dot(piece[...], xr[...].reshape(1024, 128), 1, 0, HI)
+    row_exchange(img2, j_s, j_r)
+
+    def csend(event, blk_b, lo, rows, device):
+        blk = cov_ref.at[blk_b, pl.ds(lo, rows)]
+        cp = rdma(blk, blk, v_s.at[event], v_r.at[event], device)
+        cp.start()
+        pending.append(cp)
+
+    def cwait(event, blk_b, lo, rows):
+        blk = cov_ref.at[blk_b, pl.ds(lo, rows)]
+        rdma(blk, blk, v_s.at[event], v_r.at[event], sibling).wait_recv()
+
+    yup, ydn = at(x, mod4(y + 1), z, k), at(x, mod4(y - 1), z, k)
+    zfar = at(x, y, mod4(z + 2), k)
+    yu, yd, yo = mod4(y + 1), mod4(y - 1), mod4(y + 2)
+    far = 4 * (1 - zh)
+    near = 4 * zh
+    csend(2, b, 0, 128, zfar)
+    csend(0, b, 0, 128, yup)
+    csend(1, b, 0, 128, ydn)
+
+    share_wait(gram, 0)
+    inverse = inverse_factor([gram[8 * i : 8 * i + 8, :] for i in range(16)])
+    second = dot(row_collect(img2, j_s, j_r), inverse, 1, 1, HI)
+
+    gpart2[...] = dot(second.T, second, 1, 0, HI)
+    gsib_send = rdma(
+        gpart2.at[pl.ds(pl.multiple_of(32 * x + 16 * (1 - k), 16), 16)], gsib, gs_s.at[0], gs_r.at[0], sibling
+    )
+    gsib_send.start()
+    pending.append(gsib_send)
+
+    image2[...] = second
+    holder = c == x
+
+    def out_send(i):
+        return rdma(
+            image2, last.at[lax.rem(b, 2)], o_s.at[i], o_r.at[lax.rem(b, 2)],
+            {"bin": lax.rem(b + i, 8), "row": x, "col": b // 2},
+        )
+
+    @pl.when(holder)
+    def _():
+        for i in range(1, 8):
+            out_send(i).start()
+
+        @pl.when(b // 2 == c)
+        def _():
+            last[lax.rem(b, 2)] = second
+
+        @pl.when(b // 2 != c)
+        def _():
+            out_send(0).start()
+
+    def finish_out():
+        @pl.when(holder)
+        def _():
+            for i in range(1, 8):
+                out_send(i).wait_send()
+
+            @pl.when(b // 2 != c)
+            def _():
+                out_send(0).wait_send()
+
+    late.append(finish_out)
+
+    gsib_send.wait_recv()
+    gown[...] = gpart2[pl.ds(pl.multiple_of(32 * x + 16 * k, 16), 16), :] + gsib[...]
+    gscat[here] = gown[...]
+
+    def gram2_send(i):
+        return rdma(gown, gscat.at[here], ga_s.at[1, i], ga_r.at[1, i], plane_peer(i))
+
+    def gram2_start(i, carry):
+        gram2_send(i).start()
+        return carry
+
+    lax.fori_loop(1, 16, gram2_start, 0)
+    loop_wait(gram2_send, 16)
+
     cwait(0, near + yd, 0, 128)
     csend(3, near + yd, 0, 64, yup)
     cwait(1, near + yu, 0, 128)
     csend(4, near + yu, 64, 64, ydn)
 
-    def gram_arrived(i, carry):
+    def gram2_arrived(i, carry):
         frm = lax.rem(here + 16 - i, 16)
-        rdma(gown, gscat.at[frm], ga_s.at[0, i], ga_r.at[0, i], plane_peer(i)).wait_recv()
-        return carry
-
-    lax.fori_loop(1, 16, gram_arrived, 0)
-
-    def add_slots(ref, n):
-        total = ref[0]
-        for i in range(1, n):
-            total = total + ref[i]
-        return total
-
-    gslice = x * 2 + k
-    gram[pl.ds(pl.multiple_of(16 * gslice, 16), 16), :] = add_slots(gscat, 16)
-
-    def gram_share(buf, i, first):
-        if first:
-            own = gslice
-            other = lax.rem(own + i, 8)
-            device = at(other // 2, y, z, lax.rem(other, 2))
-        else:
-            own = b
-            other = lax.rem(own + i, 8)
-            device = {"bin": other, "row": x, "col": c}
-        n = 0 if first else 1
-        blk = buf.at[pl.ds(pl.multiple_of(16 * own, 16), 16)]
-        return rdma(blk, blk, gb_s.at[n, i], gb_r.at[n, i], device)
-
-    def share_wait(buf, i, first):
-        own = gslice if first else b
-        frm = lax.rem(own + 8 - i, 8)
-        n = 0 if first else 1
-        blk = buf.at[pl.ds(pl.multiple_of(16 * frm, 16), 16)]
-        rdma(blk, blk, gb_s.at[n, i], gb_r.at[n, i], sibling).wait_recv()
-
-    for i in range(1, 8):
-        gram_share(gram, i, True).start()
-        pending.append(gram_share(gram, i, True))
-
-    def scat_arrived(i, carry):
-        frm = lax.rem(here + 16 - i, 16)
-        rdma(scat.at[frm], scat.at[frm], r_s.at[i], r_r.at[i], plane_peer(i)).wait_recv()
-        return carry
-
-    lax.fori_loop(1, 16, scat_arrived, 0)
-    zall[pl.ds(pl.multiple_of(32 * b, 32), 32), :] = add_slots(scat, 16)
-
-    def bin_share(i):
-        blk = zall.at[pl.ds(pl.multiple_of(32 * b, 32), 32)]
-        return rdma(blk, blk, z_s.at[i], z_r.at[i], {"bin": lax.rem(b + i, 8), "row": x, "col": c})
-
-    for i in range(1, 8):
-        bin_share(i).start()
-        pending.append(bin_share(i))
+        rdma(gown, gscat.at[frm], ga_s.at[1, i], ga_r.at[1, i], plane_peer(i)).wait_recv()
+        return carry
+
+    lax.fori_loop(1, 16, gram2_arrived, 0)
+    gram2[pl.ds(pl.multiple_of(32 * x + 16 * k, 16), 16), :] = add_slots(gscat, 16)
+    share_start(gram2, 1)
 
     cwait(2, far + y, 0, 128)
     csend(5, far + y, 0, 128, yup)
     csend(6, far + y, 0, 128, ydn)
 
-    for i in range(1, 8):
-        share_wait(gram, i, True)
-    inverse = inverse_factor([gram[8 * i : 8 * i + 8, :] for i in range(16)])
-    for i in range(1, 8):
-        frm = lax.rem(b + 8 - i, 8)
-        blk = zall.at[pl.ds(pl.multiple_of(32 * frm, 32), 32)]
-        rdma(blk, blk, z_s.at[i], z_r.at[i], sibling).wait_recv()
-    second = dot(zall[...], inverse, 1, 1, HI)
-    basis_ref[...] = second
-    gpart2[...] = dot(second.T, second, 1, 0, HI)
-
-    q = x * 4 + c
-    gslice_rows = pl.ds(pl.multiple_of(16 * b, 16), 16)
-    gscat2[q] = gpart2[gslice_rows, :]
-
-    def mesh_peer(i):
-        other = lax.rem(q + i, 16)
-        return {"bin": b, "row": other // 4, "col": lax.rem(other, 4)}
-
-    def gram2_send(i):
-        oq = q
-        return rdma(gscat2.at[oq], gscat2.at[oq], ga_s.at[1, i], ga_r.at[1, i], mesh_peer(i))
-
-    def gram2_start(i, carry):
-        gram2_send(i).start()
-        return carry
-
-    lax.fori_loop(1, 16, gram2_start, 0)
-    loop_wait(gram2_send, 16)
+    share_wait(gram2, 1)
+    inverse = inverse_factor([gram2[8 * i : 8 * i + 8, :] for i in range(16)])
 
     cwait(5, far + yd, 0, 128)
     csend(7, far + yd, 0, 64, yup)
     cwait(6, far + yu, 0, 128)
     csend(8, far + yu, 64, 64, ydn)
 
-    def gram2_arrived(i, carry):
-        frm = lax.rem(q + 16 - i, 16)
-        rdma(gscat2.at[frm], gscat2.at[frm], ga_s.at[1, i], ga_r.at[1, i], mesh_peer(i)).wait_recv()
-        return carry
-
-    lax.fori_loop(1, 16, gram2_arrived, 0)
-    gram2[gslice_rows, :] = add_slots(gscat2, 16)
-    for i in range(1, 8):
-        gram_share(gram2, i, False).start()
-        pending.append(gram_share(gram2, i, False))
-    for i in range(1, 8):
-        share_wait(gram2, i, False)
-    basis_ref[...] = apply_factor(gram2, basis_ref[...]) * 64.0
+    for h in (0, 1):
+        @pl.when(jnp.logical_not((c == x) & (b == 2 * c + h)))
+        def _():
+            rdma(image2, last.at[h], o_s.at[0], o_r.at[h], sibling).wait_recv()
+
+    basis_ref[...] = dot(last[...].reshape(256, 128), inverse, 1, 1, HI) * 64.0
 
     cwait(3, near + yo, 0, 64)
     cwait(4, near + yo, 64, 64)
@@ -595,6 +677,10 @@
             pltpu.VMEM((2, 256, 128), F32),
             pltpu.VMEM((16, 32, 128), F32),
             pltpu.VMEM((256, 128), F32),
+            pltpu.VMEM((4, 256, 128), F32),
+            pltpu.VMEM((4, 128, 128), F32),
+            pltpu.VMEM((128, 128), F32),
+            pltpu.VMEM((2, 128, 128), F32),
             pltpu.VMEM((128, 128), F32),
             pltpu.VMEM((16, 128), F32),
             pltpu.VMEM((16, 128), F32),
@@ -614,6 +700,9 @@
             dma((2,)), dma((2,)),
             dma((16,)), dma((16,)),
             dma((8,)), dma((8,)),
+            dma((4,)), dma((4,)),
+            dma((4,)), dma((4,)),
+            dma((8,)), dma((2,)),
             dma((1,)), dma((1,)),
             dma((2, 16)), dma((2, 16)),
             dma((2, 8)), dma((2, 8)),

time: 94.8 us -> 95.4 us (level)
  no operation moved by 1% of the time
where the time goes in v4:
time: 95.4 us; the launch traced here: 94.5 us
  Pallas kernels  89.1 us (93%)
  other arithmetic  4.1 us (4%)
    pallas_call x1, Pallas kernels, shards(): pl.pallas_call(kernel, out_shape=(jax.ShapeDtypeStruct((8, 128, 1024), BF...  89.1 us
    convert_element_type x1, other arithmetic, shards(): return (pieces.reshape(1024, 1024).astype(F32), basis_out)  4.1 us

profile of v4, /device:TPU:1, one launch (start us, length us, event | category | flops | bytes accessed | tf_op | source)
XLA Modules:
  0.0 94.5 jit_solution(16616065700440286950)
XLA Ops:
  0.6 89.1 %shard_map.59 = (bf16[8,128,1024]{2,1,0:T(8,128)(2,1)}, f32[256,128]{1,0:T(8,128)}) custom-call(bf16[128,1024]{1,0:T(8,128)(2,1)} %bitcast.6, bf16[8,1024,128]{2,1,0:T(8,128)(2,1)} %fi_hbm.1, bf16[8,1024,128]{2,1,0:T(8,128)(2,1)} %fo_hbm.1, f32[4096,128]{1,0:T(8,128)} %x0_hbm.1), custom_call_target="tpu_custom_call" | custom-call | tf_op jit(solution)/shard_map/pallas_call | solution.py:656
  89.7 0.0 copy-start
  89.8 4.1 %bitcast_convert_fusion = f32[1024,1024]{1,0:T(8,128)} fusion(bf16[8,128,1024]{2,1,0:T(8,128)(2,1)} %get-tuple-element.4), kind=kLoop, calls=%fused_computation | loop fusion | flops 1048576 | bytes 6291456 | tf_op jit(solution)/shard_map/convert_element_type | solution.py:715
  93.9 0.0 copy-done
  93.9 0.7 copy.7
Async XLA Ops:
  89.7 4.1 %copy-start = (f32[256,128]{1,0:T(8,128)S(1)}, f32[256,128]{1,0:T(8,128)}, u32[]{:S(2)}) copy-start(f32[256,128]{1,0:T(8,128)} %get-tuple-element.9) | copy-start | bytes 393220

commit v5 on v4

--- a/solution.py
+++ b/solution.py
@@ -273,6 +273,29 @@
         second_send(half, 1)
         second_send(half, 2)
 
+    def spread(ci, g, n, device):
+        blk = slab.at[ci, pl.ds(4 * g, 4)]
+        return rdma(blk, blk, x_s.at[ci, g, n], x_r.at[ci, g], device)
+
+    right, left = at(mod4(x + 1), y, z, k), at(mod4(x - 1), y, z, k)
+
+    @pl.when(is_source)
+    def _():
+        slab_local.wait()
+
+        def arrived(i, carry):
+            frm = lax.rem(here + i, 16)
+            rdma(
+                slab.at[own_ci, frm], slab.at[own_ci, frm], a_s.at[0], a_r.at[frm],
+                at(x, lax.rem(frm, 4), frm // 4, k),
+            ).wait_recv()
+            return carry
+
+        lax.fori_loop(1, 16, arrived, 0)
+        for g in range(4):
+            spread(own_ci, g, 0, right).start()
+            spread(own_ci, g, 1, left).start()
+
     weights = row_collect(img, i_s, i_r)
     part[...] = (dot_split(full[here].T, weights, 1, 0) * (1.0 / 4096)).reshape(2, 2, 256, 128)
     sibp_sends = []
@@ -282,29 +305,6 @@
         sibp_sends.append(cp)
         pending.append(cp)
 
-    def spread(ci, g, n, device):
-        blk = slab.at[ci, pl.ds(4 * g, 4)]
-        return rdma(blk, blk, x_s.at[ci, g, n], x_r.at[ci, g], device)
-
-    right, left = at(mod4(x + 1), y, z, k), at(mod4(x - 1), y, z, k)
-
-    @pl.when(is_source)
-    def _():
-        slab_local.wait()
-
-        def arrived(i, carry):
-            frm = lax.rem(here + i, 16)
-            rdma(
-                slab.at[own_ci, frm], slab.at[own_ci, frm], a_s.at[0], a_r.at[frm],
-                at(x, lax.rem(frm, 4), frm // 4, k),
-            ).wait_recv()
-            return carry
-
-        lax.fori_loop(1, 16, arrived, 0)
-        for g in range(4):
-            spread(own_ci, g, 0, right).start()
-            spread(own_ci, g, 1, left).start()
-
     def spread_roles(forward):
         for ci in (0, 1):
             d = mod4(x - (2 * zl + ci))
@@ -406,6 +406,10 @@
         second_forward(half, 2)
     spread_step(1)
     spread_step(2)
+
+    for half in (0, 1):
+        second_forward(half, 3)
+    spread_step(3)
 
     for i in range(1, 8):
         frm = lax.rem(b + 8 - i, 8)
@@ -438,10 +442,6 @@
 
     lax.fori_loop(1, 16, gram_start, 0)
     loop_wait(gram_send, 16)
-
-    for half in (0, 1):
-        second_forward(half, 3)
-    spread_step(3)
 
     def gram_share(buf, i, n):
         if n == 0:
@@ -467,14 +467,6 @@
             blk = buf.at[pl.ds(pl.multiple_of(16 * frm, 16), 16)]
             rdma(blk, blk, gb_s.at[n, i], gb_r.at[n, i], sibling).wait_recv()
 
-    def gram_arrived(i, carry):
-        frm = lax.rem(q + 16 - i, 16)
-        rdma(gscat2.at[frm], gscat2.at[frm], ga_s.at[0, i], ga_r.at[0, i], mesh_peer(i)).wait_recv()
-        return carry
-
-    lax.fori_loop(1, 16, gram_arrived, 0)
-    gram[bin_slice, :] = add_slots(gscat2, 16)
-    share_start(gram, 0)
     spread_last()
 
     def stack(places):
@@ -512,6 +504,14 @@
         cp.start()
         sib_sends.append(cp)
         pending.append(cp)
+    def gram_arrived(i, carry):
+        frm = lax.rem(q + 16 - i, 16)
+        rdma(gscat2.at[frm], gscat2.at[frm], ga_s.at[0, i], ga_r.at[0, i], mesh_peer(i)).wait_recv()
+        return carry
+
+    lax.fori_loop(1, 16, gram_arrived, 0)
+    gram[bin_slice, :] = add_slots(gscat2, 16)
+    share_start(gram, 0)
     for i in (1, 2, 3):
         frm = mod4(c - i)
         rdma(zall, xr.at[frm], y_s.at[i], y_r.at[i], sibling).wait_recv()
@@ -541,9 +541,8 @@
     yu, yd, yo = mod4(y + 1), mod4(y - 1), mod4(y + 2)
     far = 4 * (1 - zh)
     near = 4 * zh
-    csend(2, b, 0, 128, zfar)
-    csend(0, b, 0, 128, yup)
-    csend(1, b, 0, 128, ydn)
+    for event, lo, device in ((0, 0, yup), (1, 0, ydn), (8, 64, zfar), (2, 0, zfar), (9, 64, yup), (10, 64, ydn)):
+        csend(event, b, lo, 64, device)
 
     share_wait(gram, 0)
     inverse = inverse_factor([gram[8 * i : 8 * i + 8, :] for i in range(16)])
@@ -590,6 +589,20 @@
 
     late.append(finish_out)
 
+    cwait(0, near + yd, 0, 64)
+    csend(3, near + yd, 0, 32, yup)
+    csend(5, near + yd, 0, 64, zfar)
+    cwait(1, near + yu, 0, 64)
+    csend(4, near + yu, 32, 32, ydn)
+    csend(6, near + yu, 0, 64, zfar)
+    cwait(8, far + y, 64, 64)
+    csend(11, far + y, 64, 64, yup)
+    csend(12, far + y, 64, 64, ydn)
+    cwait(9, near + yd, 64, 64)
+    csend(13, near + yd, 64, 32, yup)
+    cwait(10, near + yu, 64, 64)
+    csend(14, near + yu, 96, 32, ydn)
+
     gsib_send.wait_recv()
     gown[...] = gpart2[pl.ds(pl.multiple_of(32 * x + 16 * k, 16), 16), :] + gsib[...]
     gscat[here] = gown[...]
@@ -604,10 +617,13 @@
     lax.fori_loop(1, 16, gram2_start, 0)
     loop_wait(gram2_send, 16)
 
-    cwait(0, near + yd, 0, 128)
-    csend(3, near + yd, 0, 64, yup)
-    cwait(1, near + yu, 0, 128)
-    csend(4, near + yu, 64, 64, ydn)
+    cwait(3, near + yo, 0, 32)
+    cwait(4, near + yo, 32, 32)
+    csend(7, near + yo, 0, 64, zfar)
+    cwait(11, far + yd, 64, 64)
+    csend(15, far + yd, 64, 32, yup)
+    cwait(12, far + yu, 64, 64)
+    csend(16, far + yu, 96, 32, ydn)
 
     def gram2_arrived(i, carry):
         frm = lax.rem(here + 16 - i, 16)
@@ -618,17 +634,8 @@
     gram2[pl.ds(pl.multiple_of(32 * x + 16 * k, 16), 16), :] = add_slots(gscat, 16)
     share_start(gram2, 1)
 
-    cwait(2, far + y, 0, 128)
-    csend(5, far + y, 0, 128, yup)
-    csend(6, far + y, 0, 128, ydn)
-
     share_wait(gram2, 1)
     inverse = inverse_factor([gram2[8 * i : 8 * i + 8, :] for i in range(16)])
-
-    cwait(5, far + yd, 0, 128)
-    csend(7, far + yd, 0, 64, yup)
-    cwait(6, far + yu, 0, 128)
-    csend(8, far + yu, 64, 64, ydn)
 
     for h in (0, 1):
         @pl.when(jnp.logical_not((c == x) & (b == 2 * c + h)))
@@ -637,10 +644,14 @@
 
     basis_ref[...] = dot(last[...].reshape(256, 128), inverse, 1, 1, HI) * 64.0
 
-    cwait(3, near + yo, 0, 64)
-    cwait(4, near + yo, 64, 64)
+    cwait(2, far + y, 0, 64)
+    cwait(5, far + yd, 0, 64)
+    cwait(6, far + yu, 0, 64)
     cwait(7, far + yo, 0, 64)
-    cwait(8, far + yo, 64, 64)
+    cwait(13, near + yo, 64, 32)
+    cwait(14, near + yo, 96, 32)
+    cwait(15, far + yo, 64, 32)
+    cwait(16, far + yo, 96, 32)
 
     for cp in pending:
         cp.wait_send()
@@ -695,7 +706,7 @@
             dma((8,)), dma((16,)),
             dma((2, 4, 2)), dma((2, 4)),
             dma((4,)), dma((4,)),
-            dma((9,)), dma((9,)),
+            dma((17,)), dma((17,)),
             dma((4,)), dma((4,)),
             dma((2,)), dma((2,)),
             dma((16,)), dma((16,)),

time: 95.4 us -> 94.1 us (0.986)
  no operation moved by 1% of the time
where the time goes in v5:
time: 94.1 us; the launch traced here: 94 us
  Pallas kernels  88.6 us (94%)
  other arithmetic  4.1 us (4%)
    pallas_call x1, Pallas kernels, shards(): pl.pallas_call(kernel, out_shape=(jax.ShapeDtypeStruct((8, 128, 1024), BF...  88.6 us
    convert_element_type x1, other arithmetic, shards(): return (pieces.reshape(1024, 1024).astype(F32), basis_out)  4.1 us

profile of v5, /device:TPU:1, one launch (start us, length us, event | category | flops | bytes accessed | tf_op | source)
XLA Modules:
  0.0 94.0 jit_solution(14330426610627967840)
XLA Ops:
  0.6 88.6 %shard_map.59 = (bf16[8,128,1024]{2,1,0:T(8,128)(2,1)}, f32[256,128]{1,0:T(8,128)}) custom-call(bf16[128,1024]{1,0:T(8,128)(2,1)} %bitcast.6, bf16[8,1024,128]{2,1,0:T(8,128)(2,1)} %fi_hbm.1, bf16[8,1024,128]{2,1,0:T(8,128)(2,1)} %fo_hbm.1, f32[4096,128]{1,0:T(8,128)} %x0_hbm.1), custom_call_target="tpu_custom_call" | custom-call | tf_op jit(solution)/shard_map/pallas_call | solution.py:667
  89.2 0.0 copy-start
  89.2 4.1 %bitcast_convert_fusion = f32[1024,1024]{1,0:T(8,128)} fusion(bf16[8,128,1024]{2,1,0:T(8,128)(2,1)} %get-tuple-element.4), kind=kLoop, calls=%fused_computation | loop fusion | flops 1048576 | bytes 6291456 | tf_op jit(solution)/shard_map/convert_element_type | solution.py:726
  93.3 0.0 copy-done
  93.3 0.7 copy.7
Async XLA Ops:
  89.2 4.1 %copy-start = (f32[256,128]{1,0:T(8,128)S(1)}, f32[256,128]{1,0:T(8,128)}, u32[]{:S(2)}) copy-start(f32[256,128]{1,0:T(8,128)} %get-tuple-element.9) | copy-start | bytes 393220

commit v6 on v5

--- a/solution.py
+++ b/solution.py
@@ -103,7 +103,30 @@
     def at(x_, y_, z_, k_):
         return {"bin": (z_ // 2) * 4 + y_, "row": x_, "col": lax.rem(z_, 2) * 2 + k_}
 
-    sibling = at(x, y, z, 1 - k)
+    xs, ys, zs = ([v] + [mod4(v + i) for i in (1, 2, 3)] for v in (x, y, z))
+    zhs = [zh] + [v // 2 for v in zs[1:]]
+    zls = [zl] + [v - 2 * h for v, h in zip(zs[1:], zhs[1:])]
+    zh2, zl2, ks = (zh, 1 - zh), (zl, 1 - zl), (k, 1 - k)
+
+    def plane_peer(i, dk=0):
+        return {"bin": zhs[i // 4] * 4 + ys[i % 4], "row": x, "col": zls[i // 4] * 2 + ks[dk]}
+
+    def plane_from(i):
+        return zs[-(i // 4)] * 4 + ys[-(i % 4)]
+
+    def mesh_peer(i):
+        return {"bin": b, "row": xs[i // 4], "col": zl2[i // 2 % 2] * 2 + ks[i % 2]}
+
+    def mesh_from(i):
+        return xs[-(i // 4)] * 4 + zl2[i // 2 % 2] * 2 + ks[i % 2]
+
+    def bin_peer(i):
+        return zh2[i // 4] * 4 + ys[i % 4]
+
+    def bin_from(i):
+        return zh2[i // 4] * 4 + ys[-(i % 4)]
+
+    sibling = {"bin": b, "row": x, "col": zl * 2 + (1 - k)}
     pending, late = [], []
 
     def rdma(src, dst, s, r, device):
@@ -121,25 +144,10 @@
         load.start()
 
     barrier = pltpu.get_barrier_semaphore()
-    place = b * 4 + c
-
-    def greet(i, carry):
-        other = lax.rem(place + i, 32)
-        pl.semaphore_signal(
-            barrier, inc=1, device_id={"bin": other // 4, "row": x, "col": lax.rem(other, 4)}, device_id_type=MESH
-        )
-        return carry
-
-    lax.fori_loop(1, 32, greet, 0)
-
-    def greet_rows(i, carry):
-        pl.semaphore_signal(
-            barrier, inc=1, device_id={"bin": b, "row": lax.rem(x + 1 + i // 4, 4), "col": lax.rem(i, 4)},
-            device_id_type=MESH,
-        )
-        return carry
-
-    lax.fori_loop(0, 12, greet_rows, 0)
+    for i in range(1, 32):
+        pl.semaphore_signal(barrier, inc=1, device_id=plane_peer(i // 2, i % 2), device_id_type=MESH)
+    for i in range(4, 16):
+        pl.semaphore_signal(barrier, inc=1, device_id=mesh_peer(i), device_id_type=MESH)
 
     loads[0].wait()
     loads[1].wait()
@@ -149,23 +157,22 @@
 
     def row_exchange(buf, s, r):
         for i in (2, 1, 3):
-            cp = rdma(buf.at[x], buf.at[x], s.at[i], r.at[i], at(mod4(x + i), y, z, k))
+            cp = rdma(buf.at[x], buf.at[x], s.at[i], r.at[i], {"bin": b, "row": xs[i], "col": c})
             cp.start()
             pending.append(cp)
 
     def row_collect(buf, s, r):
         for i in (1, 3, 2):
-            frm = mod4(x - i)
-            rdma(buf.at[frm], buf.at[frm], s.at[i], r.at[i], at(frm, y, z, k)).wait_recv()
+            frm = xs[-i]
+            rdma(buf.at[frm], buf.at[frm], s.at[i], r.at[i], sibling).wait_recv()
         return (buf[0] + buf[1]) + (buf[2] + buf[3])
 
     row_exchange(proj, p_s, p_r)
-    def loop_wait(send, n):
-        def one(i, carry):
-            send(i).wait_send()
-            return carry
-
-        late.append(lambda: lax.fori_loop(1, n, one, 0))
+    def start_all(send, n):
+        for i in range(1, n):
+            cp = send(i)
+            cp.start()
+            pending.append(cp)
 
     loads[2].wait()
     projected = row_collect(proj, p_s, p_r).astype(BF16)
@@ -180,18 +187,13 @@
     own_ci = lax.rem(x, 2)
 
     def slab_send(i):
-        to = lax.rem(b + i, 8)
+        to = bin_peer(i)
         return rdma(
             full.at[here, :, pl.ds(pl.multiple_of(to * 128, 128), 128)], slab.at[own_ci, here], a_s.at[i],
             a_r.at[here], {"bin": to, "row": x, "col": (x // 2) * 2 + k},
         )
 
-    def start_slab(i, carry):
-        slab_send(i).start()
-        return carry
-
-    lax.fori_loop(1, 8, start_slab, 0)
-    loop_wait(slab_send, 8)
+    start_all(slab_send, 8)
     slab_local = pltpu.make_async_copy(
         full.at[here, :, pl.ds(pl.multiple_of(b * 128, 128), 128)], slab.at[own_ci, here], l_sem.at[0]
     )
@@ -283,15 +285,9 @@
     def _():
         slab_local.wait()
 
-        def arrived(i, carry):
-            frm = lax.rem(here + i, 16)
-            rdma(
-                slab.at[own_ci, frm], slab.at[own_ci, frm], a_s.at[0], a_r.at[frm],
-                at(x, lax.rem(frm, 4), frm // 4, k),
-            ).wait_recv()
-            return carry
-
-        lax.fori_loop(1, 16, arrived, 0)
+        for i in range(1, 16):
+            frm = plane_from(i)
+            rdma(slab.at[own_ci, frm], slab.at[own_ci, frm], a_s.at[0], a_r.at[frm], sibling).wait_recv()
         for g in range(4):
             spread(own_ci, g, 0, right).start()
             spread(own_ci, g, 1, left).start()
@@ -346,10 +342,6 @@
     for half in (0, 1):
         second_forward(half, 0)
 
-    def plane_peer(i):
-        other = lax.rem(here + i, 16)
-        return at(x, lax.rem(other, 4), other // 4, k)
-
     def add_slots(ref, n):
         total = ref[0]
         for i in range(1, n):
@@ -361,20 +353,13 @@
         sibp[h] = sibp[h] + part[h, k]
 
     def scat_send(i):
-        other = lax.rem(here + i, 16)
-        oz = other // 4
-        ob = (oz // 2) * 4 + lax.rem(other, 4)
+        ob = zhs[i // 4] * 4 + ys[i % 4]
         return rdma(
-            sibp.at[lax.rem(oz, 2), pl.ds(pl.multiple_of(32 * ob, 32), 32)], scat.at[here], r_s.at[i], r_r.at[i],
+            sibp.at[zls[i // 4], pl.ds(pl.multiple_of(32 * ob, 32), 32)], scat.at[here], r_s.at[i], r_r.at[i],
             plane_peer(i),
         )
 
-    def scat_start(i, carry):
-        scat_send(i).start()
-        return carry
-
-    lax.fori_loop(1, 16, scat_start, 0)
-    loop_wait(scat_send, 16)
+    start_all(scat_send, 16)
     scat[here] = sibp[zl, pl.ds(pl.multiple_of(32 * b, 32), 32)]
 
     for half in (0, 1):
@@ -386,21 +371,16 @@
     for half in (0, 1):
         second_forward(half, 1)
 
-    def scat_arrived(i, carry):
-        frm = lax.rem(here + 16 - i, 16)
-        rdma(scat.at[frm], scat.at[frm], r_s.at[i], r_r.at[i], plane_peer(i)).wait_recv()
-        return carry
-
-    lax.fori_loop(1, 16, scat_arrived, 0)
+    for i in range(1, 16):
+        frm = plane_from(i)
+        rdma(scat.at[frm], scat.at[frm], r_s.at[i], r_r.at[i], sibling).wait_recv()
     zall[pl.ds(pl.multiple_of(32 * b, 32), 32), :] = add_slots(scat, 16)
 
     def bin_share(i):
         blk = zall.at[pl.ds(pl.multiple_of(32 * b, 32), 32)]
-        return rdma(blk, blk, z_s.at[i], z_r.at[i], {"bin": lax.rem(b + i, 8), "row": x, "col": c})
-
-    for i in range(1, 8):
-        bin_share(i).start()
-        pending.append(bin_share(i))
+        return rdma(blk, blk, z_s.at[i], z_r.at[i], {"bin": bin_peer(i), "row": x, "col": c})
+
+    start_all(bin_share, 8)
 
     for half in (0, 1):
         second_forward(half, 2)
@@ -412,7 +392,7 @@
     spread_step(3)
 
     for i in range(1, 8):
-        frm = lax.rem(b + 8 - i, 8)
+        frm = bin_from(i)
         blk = zall.at[pl.ds(pl.multiple_of(32 * frm, 32), 32)]
         rdma(blk, blk, z_s.at[i], z_r.at[i], sibling).wait_recv()
 
@@ -429,41 +409,24 @@
     bin_slice = pl.ds(pl.multiple_of(16 * b, 16), 16)
     gscat2[q] = gpart[bin_slice, :]
 
-    def mesh_peer(i):
-        other = lax.rem(q + i, 16)
-        return {"bin": b, "row": other // 4, "col": lax.rem(other, 4)}
-
     def gram_send(i):
         return rdma(gscat2.at[q], gscat2.at[q], ga_s.at[0, i], ga_r.at[0, i], mesh_peer(i))
 
-    def gram_start(i, carry):
-        gram_send(i).start()
-        return carry
-
-    lax.fori_loop(1, 16, gram_start, 0)
-    loop_wait(gram_send, 16)
+    start_all(gram_send, 16)
 
     def gram_share(buf, i, n):
         if n == 0:
             own = b
-            other = lax.rem(own + i, 8)
-            device = {"bin": other, "row": x, "col": c}
+            device = {"bin": bin_peer(i), "row": x, "col": c}
         else:
             own = x * 2 + k
-            other = lax.rem(own + i, 8)
-            device = at(other // 2, y, z, lax.rem(other, 2))
+            device = {"bin": b, "row": xs[i // 2], "col": zl * 2 + ks[i % 2]}
         blk = buf.at[pl.ds(pl.multiple_of(16 * own, 16), 16)]
         return rdma(blk, blk, gb_s.at[n, i], gb_r.at[n, i], device)
 
-    def share_start(buf, n):
+    def share_wait(buf, n):
         for i in range(1, 8):
-            gram_share(buf, i, n).start()
-            pending.append(gram_share(buf, i, n))
-
-    def share_wait(buf, n):
-        own = b if n == 0 else x * 2 + k
-        for i in range(1, 8):
-            frm = lax.rem(own + 8 - i, 8)
+            frm = bin_from(i) if n == 0 else xs[-(i // 2)] * 2 + ks[i % 2]
             blk = buf.at[pl.ds(pl.multiple_of(16 * frm, 16), 16)]
             rdma(blk, blk, gb_s.at[n, i], gb_r.at[n, i], sibling).wait_recv()
 
@@ -504,14 +467,11 @@
         cp.start()
         sib_sends.append(cp)
         pending.append(cp)
-    def gram_arrived(i, carry):
-        frm = lax.rem(q + 16 - i, 16)
-        rdma(gscat2.at[frm], gscat2.at[frm], ga_s.at[0, i], ga_r.at[0, i], mesh_peer(i)).wait_recv()
-        return carry
-
-    lax.fori_loop(1, 16, gram_arrived, 0)
+    for i in range(1, 16):
+        frm = mesh_from(i)
+        rdma(gscat2.at[frm], gscat2.at[frm], ga_s.at[0, i], ga_r.at[0, i], sibling).wait_recv()
     gram[bin_slice, :] = add_slots(gscat2, 16)
-    share_start(gram, 0)
+    start_all(lambda i: gram_share(gram, i, 0), 8)
     for i in (1, 2, 3):
         frm = mod4(c - i)
         rdma(zall, xr.at[frm], y_s.at[i], y_r.at[i], sibling).wait_recv()
@@ -557,11 +517,13 @@
 
     image2[...] = second
     holder = c == x
+    half_bin = b // 2
+    odd = b - 2 * half_bin
 
     def out_send(i):
         return rdma(
-            image2, last.at[lax.rem(b, 2)], o_s.at[i], o_r.at[lax.rem(b, 2)],
-            {"bin": lax.rem(b + i, 8), "row": x, "col": b // 2},
+            image2, last.at[odd], o_s.at[i], o_r.at[odd],
+            {"bin": bin_peer(i), "row": x, "col": half_bin},
         )
 
     @pl.when(holder)
@@ -569,11 +531,11 @@
         for i in range(1, 8):
             out_send(i).start()
 
-        @pl.when(b // 2 == c)
+        @pl.when(half_bin == c)
         def _():
-            last[lax.rem(b, 2)] = second
-
-        @pl.when(b // 2 != c)
+            last[odd] = second
+
+        @pl.when(half_bin != c)
         def _():
             out_send(0).start()
 
@@ -583,11 +545,20 @@
             for i in range(1, 8):
                 out_send(i).wait_send()
 
-            @pl.when(b // 2 != c)
+            @pl.when(half_bin != c)
             def _():
                 out_send(0).wait_send()
 
     late.append(finish_out)
+
+    gsib_send.wait_recv()
+    gown[...] = gpart2[pl.ds(pl.multiple_of(32 * x + 16 * k, 16), 16), :] + gsib[...]
+    gscat[here] = gown[...]
+
+    def gram2_send(i):
+        return rdma(gown, gscat.at[here], ga_s.at[1, i], ga_r.at[1, i], plane_peer(i))
+
+    start_all(gram2_send, 16)
 
     cwait(0, near + yd, 0, 64)
     csend(3, near + yd, 0, 32, yup)
@@ -603,19 +574,11 @@
     cwait(10, near + yu, 64, 64)
     csend(14, near + yu, 96, 32, ydn)
 
-    gsib_send.wait_recv()
-    gown[...] = gpart2[pl.ds(pl.multiple_of(32 * x + 16 * k, 16), 16), :] + gsib[...]
-    gscat[here] = gown[...]
-
-    def gram2_send(i):
-        return rdma(gown, gscat.at[here], ga_s.at[1, i], ga_r.at[1, i], plane_peer(i))
-
-    def gram2_start(i, carry):
-        gram2_send(i).start()
-        return carry
-
-    lax.fori_loop(1, 16, gram2_start, 0)
-    loop_wait(gram2_send, 16)
+    for i in range(1, 16):
+        frm = plane_from(i)
+        rdma(gown, gscat.at[frm], ga_s.at[1, i], ga_r.at[1, i], sibling).wait_recv()
+    gram2[pl.ds(pl.multiple_of(32 * x + 16 * k, 16), 16), :] = add_slots(gscat, 16)
+    start_all(lambda i: gram_share(gram2, i, 1), 8)
 
     cwait(3, near + yo, 0, 32)
     cwait(4, near + yo, 32, 32)
@@ -624,15 +587,6 @@
     csend(15, far + yd, 64, 32, yup)
     cwait(12, far + yu, 64, 64)
     csend(16, far + yu, 96, 32, ydn)
-
-    def gram2_arrived(i, carry):
-        frm = lax.rem(here + 16 - i, 16)
-        rdma(gown, gscat.at[frm], ga_s.at[1, i], ga_r.at[1, i], plane_peer(i)).wait_recv()
-        return carry
-
-    lax.fori_loop(1, 16, gram2_arrived, 0)
-    gram2[pl.ds(pl.multiple_of(32 * x + 16 * k, 16), 16), :] = add_slots(gscat, 16)
-    share_start(gram2, 1)
 
     share_wait(gram2, 1)
     inverse = inverse_factor([gram2[8 * i : 8 * i + 8, :] for i in range(16)])

time: 94.1 us -> 92.3 us (0.981)
  Pallas kernels: 88.6 us -> 86.8 us
    pallas_call x1, Pallas kernels: 88.6 us -> 86.8 us  [shards(): pl.pallas_call(kernel, out_shape=(jax.ShapeDtypeStruct((8, 128, 1024), BF...]
where the time goes in v6:
time: 92.3 us; the launch traced here: 92.2 us
  Pallas kernels  86.8 us (94%)
  other arithmetic  4.1 us (4%)
    pallas_call x1, Pallas kernels, shards(): pl.pallas_call(kernel, out_shape=(jax.ShapeDtypeStruct((8, 128, 1024), BF...  86.8 us
    convert_element_type x1, other arithmetic, shards(): return (pieces.reshape(1024, 1024).astype(F32), basis_out)  4.1 us

profile of v6, /device:TPU:1, one launch (start us, length us, event | category | flops | bytes accessed | tf_op | source)
XLA Modules:
  0.0 92.2 jit_solution(1097241938879527045)
XLA Ops:
  0.6 86.8 %shard_map.59 = (bf16[8,128,1024]{2,1,0:T(8,128)(2,1)}, f32[256,128]{1,0:T(8,128)}) custom-call(bf16[128,1024]{1,0:T(8,128)(2,1)} %bitcast.6, bf16[8,1024,128]{2,1,0:T(8,128)(2,1)} %fi_hbm.1, bf16[8,1024,128]{2,1,0:T(8,128)(2,1)} %fo_hbm.1, f32[4096,128]{1,0:T(8,128)} %x0_hbm.1), custom_call_target="tpu_custom_call" | custom-call | tf_op jit(solution)/shard_map/pallas_call | solution.py:621
  87.4 0.0 copy-start
  87.4 4.1 %bitcast_convert_fusion = f32[1024,1024]{1,0:T(8,128)} fusion(bf16[8,128,1024]{2,1,0:T(8,128)(2,1)} %get-tuple-element.4), kind=kLoop, calls=%fused_computation | loop fusion | flops 1048576 | bytes 6291456 | tf_op jit(solution)/shard_map/convert_element_type | solution.py:680
  91.5 0.0 copy-done
  91.5 0.7 copy.7
Async XLA Ops:
  87.4 4.1 %copy-start = (f32[256,128]{1,0:T(8,128)S(1)}, f32[256,128]{1,0:T(8,128)}, u32[]{:S(2)}) copy-start(f32[256,128]{1,0:T(8,128)} %get-tuple-element.9) | copy-start | bytes 393220

commit v7 on v6

--- a/solution.py
+++ b/solution.py
@@ -87,9 +87,9 @@
 def kernel(
     snap_hbm, fi_hbm, fo_hbm, x0_hbm, cov_ref, basis_ref,
     snap, fi, fo, x0, proj, full, slab, acc, sibc, piece, img, part, sibp, scat, zall, xr, img2, image2, last,
-    gpart, gsib, gown, gscat, gram, gpart2, gscat2, gram2, in_sem,
+    gx, gsib, gown, gscat, gpart2, gram2, in_sem,
     p_s, p_r, g_s, g_r, a_s, a_r, x_s, x_r, c_s, c_r, v_s, v_r, i_s, i_r, q_s, q_r, r_s, r_r, z_s, z_r,
-    y_s, y_r, j_s, j_r, o_s, o_r, gs_s, gs_r, ga_s, ga_r, gb_s, gb_r, l_sem,
+    y_s, y_r, j_s, j_r, o_s, o_r, gs_s, gs_r, ga_s, ga_r, gb_s, gb_r, h_s, h_r, l_sem,
 ):
     b = lax.axis_index("bin")
     x = lax.axis_index("row")
@@ -402,33 +402,17 @@
     for i in (2, 1, 3):
         col_share(i).start()
         pending.append(col_share(i))
-    first = zall[...]
-    xr[c] = first
-    gpart[...] = dot(first.T, first, 1, 0, HI)
-    q = x * 4 + c
-    bin_slice = pl.ds(pl.multiple_of(16 * b, 16), 16)
-    gscat2[q] = gpart[bin_slice, :]
-
-    def gram_send(i):
-        return rdma(gscat2.at[q], gscat2.at[q], ga_s.at[0, i], ga_r.at[0, i], mesh_peer(i))
-
-    start_all(gram_send, 16)
-
-    def gram_share(buf, i, n):
-        if n == 0:
-            own = b
-            device = {"bin": bin_peer(i), "row": x, "col": c}
-        else:
-            own = x * 2 + k
-            device = {"bin": b, "row": xs[i // 2], "col": zl * 2 + ks[i % 2]}
-        blk = buf.at[pl.ds(pl.multiple_of(16 * own, 16), 16)]
-        return rdma(blk, blk, gb_s.at[n, i], gb_r.at[n, i], device)
-
-    def share_wait(buf, n):
+    xr[c] = zall[...]
+
+    def gram_share(i):
+        blk = gram2.at[pl.ds(pl.multiple_of(16 * (x * 2 + k), 16), 16)]
+        return rdma(blk, blk, gb_s.at[i], gb_r.at[i], {"bin": b, "row": xs[i // 2], "col": zl * 2 + ks[i % 2]})
+
+    def share_wait():
         for i in range(1, 8):
-            frm = bin_from(i) if n == 0 else xs[-(i // 2)] * 2 + ks[i % 2]
-            blk = buf.at[pl.ds(pl.multiple_of(16 * frm, 16), 16)]
-            rdma(blk, blk, gb_s.at[n, i], gb_r.at[n, i], sibling).wait_recv()
+            frm = xs[-(i // 2)] * 2 + ks[i % 2]
+            blk = gram2.at[pl.ds(pl.multiple_of(16 * frm, 16), 16)]
+            rdma(blk, blk, gb_s.at[i], gb_r.at[i], sibling).wait_recv()
 
     spread_last()
 
@@ -454,6 +438,14 @@
     lhs = stack(early)
     for n in range(4):
         acc[n] = multiply(early, lhs, n)
+
+    for i in (1, 2, 3):
+        frm = mod4(c - i)
+        rdma(zall, xr.at[frm], y_s.at[i], y_r.at[i], sibling).wait_recv()
+    rows_image = xr[...].reshape(1024, 128)
+    gx[x] = dot(rows_image.T, rows_image, 1, 0, HI)
+    row_exchange(gx, h_s, h_r)
+
     for half in (0, 1):
         for t in range(4):
             second_last(half, t)
@@ -467,14 +459,6 @@
         cp.start()
         sib_sends.append(cp)
         pending.append(cp)
-    for i in range(1, 16):
-        frm = mesh_from(i)
-        rdma(gscat2.at[frm], gscat2.at[frm], ga_s.at[0, i], ga_r.at[0, i], sibling).wait_recv()
-    gram[bin_slice, :] = add_slots(gscat2, 16)
-    start_all(lambda i: gram_share(gram, i, 0), 8)
-    for i in (1, 2, 3):
-        frm = mod4(c - i)
-        rdma(zall, xr.at[frm], y_s.at[i], y_r.at[i], sibling).wait_recv()
     scaling = 1.0 / 4096
     mine = pl.ds(pl.multiple_of(k * 128, 128), 128)
     for n in range(4):
@@ -504,7 +488,7 @@
     for event, lo, device in ((0, 0, yup), (1, 0, ydn), (8, 64, zfar), (2, 0, zfar), (9, 64, yup), (10, 64, ydn)):
         csend(event, b, lo, 64, device)
 
-    share_wait(gram, 0)
+    gram = row_collect(gx, h_s, h_r)
     inverse = inverse_factor([gram[8 * i : 8 * i + 8, :] for i in range(16)])
     second = dot(row_collect(img2, j_s, j_r), inverse, 1, 1, HI)
 
@@ -515,6 +499,15 @@
     gsib_send.start()
     pending.append(gsib_send)
 
+    gsib_send.wait_recv()
+    gown[...] = gpart2[pl.ds(pl.multiple_of(32 * x + 16 * k, 16), 16), :] + gsib[...]
+    gscat[here] = gown[...]
+
+    def gram2_send(i):
+        return rdma(gown, gscat.at[here], ga_s.at[i], ga_r.at[i], plane_peer(i))
+
+    start_all(gram2_send, 16)
+
     image2[...] = second
     holder = c == x
     half_bin = b // 2
@@ -550,15 +543,6 @@
                 out_send(0).wait_send()
 
     late.append(finish_out)
-
-    gsib_send.wait_recv()
-    gown[...] = gpart2[pl.ds(pl.multiple_of(32 * x + 16 * k, 16), 16), :] + gsib[...]
-    gscat[here] = gown[...]
-
-    def gram2_send(i):
-        return rdma(gown, gscat.at[here], ga_s.at[1, i], ga_r.at[1, i], plane_peer(i))
-
-    start_all(gram2_send, 16)
 
     cwait(0, near + yd, 0, 64)
     csend(3, near + yd, 0, 32, yup)
@@ -576,9 +560,9 @@
 
     for i in range(1, 16):
         frm = plane_from(i)
-        rdma(gown, gscat.at[frm], ga_s.at[1, i], ga_r.at[1, i], sibling).wait_recv()
+        rdma(gown, gscat.at[frm], ga_s.at[i], ga_r.at[i], sibling).wait_recv()
     gram2[pl.ds(pl.multiple_of(32 * x + 16 * k, 16), 16), :] = add_slots(gscat, 16)
-    start_all(lambda i: gram_share(gram2, i, 1), 8)
+    start_all(gram_share, 8)
 
     cwait(3, near + yo, 0, 32)
     cwait(4, near + yo, 32, 32)
@@ -588,7 +572,7 @@
     cwait(12, far + yu, 64, 64)
     csend(16, far + yu, 96, 32, ydn)
 
-    share_wait(gram2, 1)
+    share_wait()
     inverse = inverse_factor([gram2[8 * i : 8 * i + 8, :] for i in range(16)])
 
     for h in (0, 1):
@@ -646,13 +630,11 @@
             pltpu.VMEM((4, 128, 128), F32),
             pltpu.VMEM((128, 128), F32),
             pltpu.VMEM((2, 128, 128), F32),
-            pltpu.VMEM((128, 128), F32),
+            pltpu.VMEM((4, 128, 128), F32),
             pltpu.VMEM((16, 128), F32),
             pltpu.VMEM((16, 128), F32),
             pltpu.VMEM((16, 16, 128), F32),
             pltpu.VMEM((128, 128), F32),
-            pltpu.VMEM((128, 128), F32),
-            pltpu.VMEM((16, 16, 128), F32),
             pltpu.VMEM((128, 128), F32),
             dma((4,)),
             dma((4,)), dma((4,)),
@@ -669,8 +651,9 @@
             dma((4,)), dma((4,)),
             dma((8,)), dma((2,)),
             dma((1,)), dma((1,)),
-            dma((2, 16)), dma((2, 16)),
-            dma((2, 8)), dma((2, 8)),
+            dma((16,)), dma((16,)),
+            dma((8,)), dma((8,)),
+            dma((4,)), dma((4,)),
             dma((1,)),
         ],
         compiler_params=pltpu.CompilerParams(

time: 92.3 us -> 92.8 us (level)
  the two profiles are of different devices: /device:TPU:1 before, /device:TPU:33 now
where the time goes in v7:
time: 92.8 us; the launch traced here: 92.6 us
  Pallas kernels  87.2 us (94%)
  other arithmetic  4.1 us (4%)
    pallas_call x1, Pallas kernels, shards(): pl.pallas_call(kernel, out_shape=(jax.ShapeDtypeStruct((8, 128, 1024), BF...  87.2 us
    convert_element_type x1, other arithmetic, shards(): return (pieces.reshape(1024, 1024).astype(F32), basis_out)  4.1 us

profile of v7, /device:TPU:33, one launch (start us, length us, event | category | flops | bytes accessed | tf_op | source)
XLA Modules:
  0.0 92.6 jit_solution(8492922085173804985)
XLA Ops:
  0.6 87.2 %shard_map.59 = (bf16[8,128,1024]{2,1,0:T(8,128)(2,1)}, f32[256,128]{1,0:T(8,128)}) custom-call(bf16[128,1024]{1,0:T(8,128)(2,1)} %bitcast.6, bf16[8,1024,128]{2,1,0:T(8,128)(2,1)} %fi_hbm.1, bf16[8,1024,128]{2,1,0:T(8,128)(2,1)} %fo_hbm.1, f32[4096,128]{1,0:T(8,128)} %x0_hbm.1), custom_call_target="tpu_custom_call" | custom-call | tf_op jit(solution)/shard_map/pallas_call | solution.py:605
  87.8 0.0 copy-start
  87.8 4.1 %bitcast_convert_fusion = f32[1024,1024]{1,0:T(8,128)} fusion(bf16[8,128,1024]{2,1,0:T(8,128)(2,1)} %get-tuple-element.4), kind=kLoop, calls=%fused_computation | loop fusion | flops 1048576 | bytes 6291456 | tf_op jit(solution)/shard_map/convert_element_type | solution.py:663
  92.0 0.0 copy-done
  92.0 0.7 copy.7
Async XLA Ops:
  87.8 4.1 %copy-start = (f32[256,128]{1,0:T(8,128)S(1)}, f32[256,128]{1,0:T(8,128)}, u32[]{:S(2)}) copy-start(f32[256,128]{1,0:T(8,128)} %get-tuple-element.9) | copy-start | bytes 393220

commit v8 on v7

--- a/solution.py
+++ b/solution.py
@@ -266,6 +266,25 @@
     img[x] = dot_split(full[here], x0[...], 1, 0)
     row_exchange(img, i_s, i_r)
 
+    def spread(ci, g, n, device):
+        blk = slab.at[ci, pl.ds(4 * g, 4)]
+        return rdma(blk, blk, x_s.at[ci, g, n], x_r.at[ci, g], device)
+
+    right, left = at(mod4(x + 1), y, z, k), at(mod4(x - 1), y, z, k)
+
+    @pl.when(is_source)
+    def _():
+        slab_local.wait()
+
+        for dz in range(4):
+            for i in range(4 * dz, 4 * dz + 4):
+                if i:
+                    frm = plane_from(i)
+                    rdma(slab.at[own_ci, frm], slab.at[own_ci, frm], a_s.at[0], a_r.at[frm], sibling).wait_recv()
+            spread(own_ci, zs[-dz], 0, right).start()
+            spread(own_ci, zs[-dz], 1, left).start()
+
+
     for half in (0, 1):
         u, v = ring(half)
         gwait(half, 0, mod4(u - 1), v, 0, 64)
@@ -274,23 +293,6 @@
         gsend(half, 3, mod4(u + 1), v, 32, 32, mod4(u - 1), v)
         second_send(half, 1)
         second_send(half, 2)
-
-    def spread(ci, g, n, device):
-        blk = slab.at[ci, pl.ds(4 * g, 4)]
-        return rdma(blk, blk, x_s.at[ci, g, n], x_r.at[ci, g], device)
-
-    right, left = at(mod4(x + 1), y, z, k), at(mod4(x - 1), y, z, k)
-
-    @pl.when(is_source)
-    def _():
-        slab_local.wait()
-
-        for i in range(1, 16):
-            frm = plane_from(i)
-            rdma(slab.at[own_ci, frm], slab.at[own_ci, frm], a_s.at[0], a_r.at[frm], sibling).wait_recv()
-        for g in range(4):
-            spread(own_ci, g, 0, right).start()
-            spread(own_ci, g, 1, left).start()
 
     weights = row_collect(img, i_s, i_r)
     part[...] = (dot_split(full[here].T, weights, 1, 0) * (1.0 / 4096)).reshape(2, 2, 256, 128)
@@ -312,8 +314,8 @@
 
             @pl.when(passes_on)
             def _():
-                spread(ci, g, 0, right).wait_recv()
-                spread(ci, g, 0, left if ci == 0 else right).start()
+                spread(ci, zs[-g], 0, right).wait_recv()
+                spread(ci, zs[-g], 0, left if ci == 0 else right).start()
 
     def spread_last():
         for ci, receives in spread_roles(False):
@@ -370,6 +372,7 @@
     spread_step(0)
     for half in (0, 1):
         second_forward(half, 1)
+    spread_step(1)
 
     for i in range(1, 16):
         frm = plane_from(i)
@@ -384,12 +387,11 @@
 
     for half in (0, 1):
         second_forward(half, 2)
-    spread_step(1)
     spread_step(2)
+    spread_step(3)
 
     for half in (0, 1):
         second_forward(half, 3)
-    spread_step(3)
 
     for i in range(1, 8):
         frm = bin_from(i)
@@ -492,58 +494,6 @@
     inverse = inverse_factor([gram[8 * i : 8 * i + 8, :] for i in range(16)])
     second = dot(row_collect(img2, j_s, j_r), inverse, 1, 1, HI)
 
-    gpart2[...] = dot(second.T, second, 1, 0, HI)
-    gsib_send = rdma(
-        gpart2.at[pl.ds(pl.multiple_of(32 * x + 16 * (1 - k), 16), 16)], gsib, gs_s.at[0], gs_r.at[0], sibling
-    )
-    gsib_send.start()
-    pending.append(gsib_send)
-
-    gsib_send.wait_recv()
-    gown[...] = gpart2[pl.ds(pl.multiple_of(32 * x + 16 * k, 16), 16), :] + gsib[...]
-    gscat[here] = gown[...]
-
-    def gram2_send(i):
-        return rdma(gown, gscat.at[here], ga_s.at[i], ga_r.at[i], plane_peer(i))
-
-    start_all(gram2_send, 16)
-
-    image2[...] = second
-    holder = c == x
-    half_bin = b // 2
-    odd = b - 2 * half_bin
-
-    def out_send(i):
-        return rdma(
-            image2, last.at[odd], o_s.at[i], o_r.at[odd],
-            {"bin": bin_peer(i), "row": x, "col": half_bin},
-        )
-
-    @pl.when(holder)
-    def _():
-        for i in range(1, 8):
-            out_send(i).start()
-
-        @pl.when(half_bin == c)
-        def _():
-            last[odd] = second
-
-        @pl.when(half_bin != c)
-        def _():
-            out_send(0).start()
-
-    def finish_out():
-        @pl.when(holder)
-        def _():
-            for i in range(1, 8):
-                out_send(i).wait_send()
-
-            @pl.when(half_bin != c)
-            def _():
-                out_send(0).wait_send()
-
-    late.append(finish_out)
-
     cwait(0, near + yd, 0, 64)
     csend(3, near + yd, 0, 32, yup)
     csend(5, near + yd, 0, 64, zfar)
@@ -557,6 +507,58 @@
     csend(13, near + yd, 64, 32, yup)
     cwait(10, near + yu, 64, 64)
     csend(14, near + yu, 96, 32, ydn)
+
+    gpart2[...] = dot(second.T, second, 1, 0, HI)
+    gsib_send = rdma(
+        gpart2.at[pl.ds(pl.multiple_of(32 * x + 16 * (1 - k), 16), 16)], gsib, gs_s.at[0], gs_r.at[0], sibling
+    )
+    gsib_send.start()
+    pending.append(gsib_send)
+
+    gsib_send.wait_recv()
+    gown[...] = gpart2[pl.ds(pl.multiple_of(32 * x + 16 * k, 16), 16), :] + gsib[...]
+    gscat[here] = gown[...]
+
+    def gram2_send(i):
+        return rdma(gown, gscat.at[here], ga_s.at[i], ga_r.at[i], plane_peer(i))
+
+    start_all(gram2_send, 16)
+
+    image2[...] = second
+    holder = c == x
+    half_bin = b // 2
+    odd = b - 2 * half_bin
+
+    def out_send(i):
+        return rdma(
+            image2, last.at[odd], o_s.at[i], o_r.at[odd],
+            {"bin": bin_peer(i), "row": x, "col": half_bin},
+        )
+
+    @pl.when(holder)
+    def _():
+        for i in range(1, 8):
+            out_send(i).start()
+
+        @pl.when(half_bin == c)
+        def _():
+            last[odd] = second
+
+        @pl.when(half_bin != c)
+        def _():
+            out_send(0).start()
+
+    def finish_out():
+        @pl.when(holder)
+        def _():
+            for i in range(1, 8):
+                out_send(i).wait_send()
+
+            @pl.when(half_bin != c)
+            def _():
+                out_send(0).wait_send()
+
+    late.append(finish_out)
 
     for i in range(1, 16):
         frm = plane_from(i)

time: 92.8 us -> 90.7 us (0.977)
  the two profiles are of different devices: /device:TPU:33 before, /device:TPU:1 now
where the time goes in v8:
time: 90.7 us; the launch traced here: 90.6 us
  Pallas kernels  85.2 us (94%)
  other arithmetic  4.1 us (5%)
    pallas_call x1, Pallas kernels, shards(): pl.pallas_call(kernel, out_shape=(jax.ShapeDtypeStruct((8, 128, 1024), BF...  85.2 us
    convert_element_type x1, other arithmetic, shards(): return (pieces.reshape(1024, 1024).astype(F32), basis_out)  4.1 us

profile of v8, /device:TPU:1, one launch (start us, length us, event | category | flops | bytes accessed | tf_op | source)
XLA Modules:
  0.0 90.6 jit_solution(18096939792472923525)
XLA Ops:
  0.6 85.2 %shard_map.59 = (bf16[8,128,1024]{2,1,0:T(8,128)(2,1)}, f32[256,128]{1,0:T(8,128)}) custom-call(bf16[128,1024]{1,0:T(8,128)(2,1)} %bitcast.6, bf16[8,1024,128]{2,1,0:T(8,128)(2,1)} %fi_hbm.1, bf16[8,1024,128]{2,1,0:T(8,128)(2,1)} %fo_hbm.1, f32[4096,128]{1,0:T(8,128)} %x0_hbm.1), custom_call_target="tpu_custom_call" | custom-call | tf_op jit(solution)/shard_map/pallas_call | solution.py:607
  85.8 0.0 copy-start
  85.8 4.1 %bitcast_convert_fusion = f32[1024,1024]{1,0:T(8,128)} fusion(bf16[8,128,1024]{2,1,0:T(8,128)(2,1)} %get-tuple-element.4), kind=kLoop, calls=%fused_computation | loop fusion | flops 1048576 | bytes 6291456 | tf_op jit(solution)/shard_map/convert_element_type | solution.py:665
  89.9 0.0 copy-done
  89.9 0.7 copy.7
Async XLA Ops:
  85.8 4.1 %copy-start = (f32[256,128]{1,0:T(8,128)S(1)}, f32[256,128]{1,0:T(8,128)}, u32[]{:S(2)}) copy-start(f32[256,128]{1,0:T(8,128)} %get-tuple-element.9) | copy-start | bytes 393220
